TPU v7x, 32 devices: a whole 2x2x4 slice. The times are simulated.
32 devices in a mesh: comp: 2 (over y), gy: 4 (over z), gx: 4 (over x, core).
Axes of the slice: x: 2, y: 2, z: 4, core: 2. Of those that a mesh axis runs over, the one named last changes fastest.
Arguments:
- spectra: float32 [32, 36, 16, 512], P('comp', None, 'gy', 'gx'), may hold values from 0.05 to 2
- wind_field: float32 [2, 16, 512], P(None, 'gy', 'gx'), may hold values from -5 to 5
- sea_mask: int32 [16, 512], P('gy', 'gx'), may hold values 0 or 1
- first_layer: bfloat16 [1152, 1024], replicated, may hold values from -0.1875 to 0.1875
- second_layer: bfloat16 [1024, 1152], replicated, may hold values from -0.1875 to 0.1875
- ocean_state: float32 [4, 16, 16, 512], P(None, None, 'gy', 'gx'), may hold values from -4 to 4
- current_blocks: float32 [16, 2, 512, 128], P('gy', None, 'gx'), may hold values from 0 to 1
- current_rows: int32 [16, 2, 4], P('gy', None, 'gx'), may hold values from 0 to 15, as said below
- stress_blocks: float32 [16, 2, 512, 128], P('gy', None, 'gx'), may hold values from 0 to 1
- stress_rows: int32 [16, 2, 4], P('gy', None, 'gx'), may hold values from 0 to 15, as said below
Outputs:
- spectra_next: float32 [32, 36, 16, 512], P('comp', None, 'gy', 'gx')
- ocean_next: float32 [4, 16, 16, 512], P(None, None, 'gy', 'gx')
Inputs may be any that keep to these rules, and one draw needn't show every extreme that they name: `current_rows`: entry [r, b, t] is the source row read by block b of destination row r in column tile t; it lies within one row of r, and both r - 1 and r + 1 occur. `stress_rows`: entry [r, b, t] is the source row read by block b of destination row r in column tile t; it lies within one row of r, and both r - 1 and r + 1 occur.
All inputs are finite; a program needn't handle non-finite values. No bound on the sum of `sea_mask` on one device may be relied on, other than what follows from the above.
Results may differ from a plain program's by a relative error of at most 0.0023.
Values may be sent and summed in bfloat16 or wider, within the bound.
A program may use at most 64 MiB of HBM per device.

v0:
```python
import numpy as np

import jax
import jax.numpy as jnp
from jax import lax
from jax.experimental import pallas as pl
from jax.experimental.pallas import tpu as pltpu
from jax.sharding import PartitionSpec as P

CURRENT_GAIN = 0.08
WIND_GAIN = 0.06
DECAY_GAIN = 0.03
NONLINEAR_GAIN = 0.3
THERMAL = 0.2
HALINE = 0.8
CORIOLIS = 0.1
PRESSURE_GAIN = 0.2
LATERAL_MIX = 0.1
VERTICAL_MIX = 0.2
ADVECTION = 0.3
STRESS_GAIN = 150.0

STEPS = 2
ROWS = 4
COLS = 128
HALF = 64
CELLS = ROWS * HALF
TILE = 128
TILES = 9
OWN = 4
PAD = 8
GROUPS = ((0, 1), (5, 6), (4,), (2, 3), (7, 8))
SENDERS = (1, 0, 2, 4, 3)
LAST_GROUPS = ((5, 6), (7, 8), (4,), (0, 1), (2, 3))
VMEM_LIMIT = 56 * 1024 * 1024


def tables(total, directions):
    index = np.arange(total, dtype=np.float64)
    group = 0.4 * np.exp(-3.0 * index / (total - 1))
    ratio = np.exp(2.0 * index / (total - 1) - 1.0)
    angles = 2.0 * np.pi * np.arange(directions) / directions
    cosines, sines = np.cos(angles), np.sin(angles)
    full = np.zeros((8, total, directions))
    full[0] = group[:, None] * cosines
    full[1] = group[:, None] * sines
    full[2] = cosines
    full[3] = sines
    full[4] = WIND_GAIN * 4.0 * group[:, None]
    full[5] = ratio[:, None]
    tiled = full.reshape(8, TILES, TILE).transpose(1, 0, 2)
    swapped = np.concatenate([tiled[5:], tiled[4:5], tiled[:4]])
    return np.stack([tiled, swapped]).astype(np.float32)


def mirror(t):
    return 4 if t == 4 else (t + 5) % 10


def kernel(
    spectra, first, second, table, ocean, wind, mask, cblocks, sblocks, crows, srows,
    out, o_out,
    spec, w1, w2, tab, oc, wnd, msk, cb, sb,
    state, prop, rate, p16, part, hidden, sums, cells, gain, back, squared, small, small_t,
    y_out, y_in, z1_out, z1_in, zf_in, es_out, es_in, ed_out, ed_in, ep_out, ep_in, el,
    z2_out, z2_in, e2d_out, e2d_in, e2p_out, e2p_in,
    oz_out, oz_in, ocat, ox_out, ox_in, st_out, st_in, st_full, sz_in, f_out, f_in,
    load, oz_send, oz_recv, ox_send, ox_recv, y_send, y_recv, z1_send, z1_recv,
    zf_send, zf_recv, e1_send, e1_recv, z2_send, z2_recv, e2_send, e2_recv,
    s_send, s_recv, f_send, f_recv,
):
    f32, b16 = jnp.float32, jnp.bfloat16
    me = lax.axis_index("comp")
    other = 1 - me
    gy, ny = lax.axis_index("gy"), lax.axis_size("gy")
    gx, nx = lax.axis_index("gx"), lax.axis_size("gx")
    comps = spectra.shape[0]
    mesh_ids = pl.DeviceIdType.MESH

    def local(source, target, n):
        return pltpu.make_async_copy(source, target, load.at[n])

    own_at = pl.multiple_of(me * 5 * TILE, TILE)
    far_at = pl.multiple_of(other * 5 * TILE, TILE)
    half_at = pl.multiple_of(me * HALF, HALF)
    spec_load = local(spectra, spec.at[pl.ds(HALF, comps)], 0)
    ocean_load = local(ocean, oc, 1)
    wind_load = local(wind, wnd, 2)
    mask_load = local(mask, msk, 3)
    table_load = local(table.at[me], tab, 4)
    cb_load = local(cblocks.at[:, :, pl.ds(half_at, HALF), :], cb, 5)
    sb_load = local(sblocks, sb, 6)
    w1_loads = [
        local(first.at[pl.ds(own_at, 512)], w1.at[pl.ds(0, 512)], 7),
        local(first.at[pl.ds(512, 128)], w1.at[pl.ds(512, 128)], 8),
        local(first.at[pl.ds(far_at, 512)], w1.at[pl.ds(640, 512)], 9),
    ]
    w2_loads = [
        local(second.at[:, pl.ds(own_at, 512)], w2.at[:, pl.ds(0, 512)], 10),
        local(second.at[:, pl.ds(512, 128)], w2.at[:, pl.ds(512, 128)], 11),
        local(second.at[:, pl.ds(far_at, 512)], w2.at[:, pl.ds(640, 512)], 12),
    ]
    all_loads = [ocean_load, spec_load, wind_load, mask_load, table_load, cb_load]
    all_loads += w1_loads + w2_loads + [sb_load]
    for copy in all_loads:
        copy.start()

    for ref in (es_in, ed_in, e2d_in, sz_in, ox_in, oz_in):
        ref[...] = jnp.zeros_like(ref)

    has_s, has_n = gy > 0, gy < ny - 1
    has_w, has_e = gx > 0, gx < nx - 1
    south = {"gy": lax.rem(gy + ny - 1, ny)}
    north = {"gy": lax.rem(gy + 1, ny)}
    west = {"gx": lax.rem(gx + nx - 1, nx)}
    east = {"gx": lax.rem(gx + 1, nx)}
    pair = {"comp": other}
    far_gx = gx + 2 * me - 1
    has_far = jnp.logical_and(far_gx >= 0, far_gx < nx)
    diag = {"comp": other, "gx": lax.rem(far_gx + nx, nx)}
    same_gx = gx + 1 - 2 * me
    has_same = jnp.logical_and(same_gx >= 0, same_gx < nx)
    same = {"gx": lax.rem(same_gx + nx, nx)}

    barrier = pltpu.get_barrier_semaphore()
    greet = ((has_s, south), (has_n, north), (has_w, west), (has_e, east), (has_far, diag))
    for there, place in greet:
        @pl.when(there)
        def _(place=place):
            pl.semaphore_signal(barrier, inc=1, device_id=place, device_id_type=mesh_ids)
    pl.semaphore_signal(barrier, inc=1, device_id=pair, device_id_type=mesh_ids)

    def remote(source, target, send, recv, where):
        return pltpu.make_async_remote_copy(
            src_ref=source, dst_ref=target, send_sem=send, recv_sem=recv,
            device_id=where, device_id_type=mesh_ids,
        )

    ocean_n = remote(oz_out.at[0], oz_in.at[0], oz_send.at[0], oz_recv.at[0], north)
    ocean_s = remote(oz_out.at[1], oz_in.at[1], oz_send.at[1], oz_recv.at[1], south)
    ocean_e = remote(
        ox_out.at[pl.ds(120, 8)], ox_in.at[0, pl.ds(120, 8)], ox_send.at[0], ox_recv.at[0], east
    )
    ocean_w = remote(
        ox_out.at[pl.ds(0, 8)], ox_in.at[1, pl.ds(0, 8)], ox_send.at[1], ox_recv.at[1], west
    )
    swap = [
        remote(y_out.at[r], y_in.at[r], y_send.at[r], y_recv.at[r], pair) for r in range(ROWS)
    ]
    z1_n = remote(z1_out.at[0], z1_in.at[0], z1_send.at[0], z1_recv.at[0], north)
    z1_s = remote(z1_out.at[1], z1_in.at[1], z1_send.at[1], z1_recv.at[1], south)
    zf_n = remote(y_in.at[ROWS - 1], zf_in.at[0], zf_send.at[0], zf_recv.at[0], north)
    zf_s = remote(y_in.at[0], zf_in.at[1], zf_send.at[1], zf_recv.at[1], south)
    e_same = remote(es_out, es_in, e1_send.at[0], e1_recv.at[0], same)
    e_diag = remote(ed_out, ed_in, e1_send.at[1], e1_recv.at[1], diag)
    e_pair = remote(ep_out, ep_in, e1_send.at[2], e1_recv.at[2], pair)

    def span(tiles):
        return pl.ds(tiles[0], len(tiles))

    z2 = []
    e2 = []
    for g, tiles in enumerate(GROUPS):
        part_of = span(tiles)
        z2.append([
            remote(
                z2_out.at[d, part_of], z2_in.at[d, part_of],
                z2_send.at[d, g], z2_recv.at[d, g], (north, south)[d],
            )
            for d in range(2)
        ])
        there = span(tuple(sorted(mirror(t) for t in tiles)))
        e2.append([
            remote(
                e2d_out.at[part_of], e2d_in.at[there], e2_send.at[0, g], e2_recv.at[0, g], diag
            ),
            remote(
                e2p_out.at[part_of], e2p_in.at[there], e2_send.at[1, g], e2_recv.at[1, g], pair
            ),
        ])
    stress_pair = remote(st_out, st_in, s_send.at[0], s_recv.at[0], pair)
    stress_n = remote(st_full, sz_in.at[0], s_send.at[1], s_recv.at[1], north)
    stress_s = remote(st_full, sz_in.at[1], s_send.at[2], s_recv.at[2], south)
    final_parts = (pl.ds(0, 2), pl.ds(2, 2), pl.ds(4, 1))
    final = [
        remote(f_out.at[p], f_in.at[p], f_send.at[n], f_recv.at[n], pair)
        for n, p in enumerate(final_parts)
    ]

    def when(condition, *actions):
        @pl.when(condition)
        def _():
            for action in actions:
                action()

    state[...] = jnp.zeros_like(state)
    spec[:HALF] = jnp.zeros((HALF, ROWS, COLS), f32)
    spec[HALF + comps :] = jnp.zeros((HALF, ROWS, COLS), f32)

    ocean_load.wait()
    oz_out[0] = oc[:, ROWS - 1, :]
    oz_out[1] = oc[:, 0, :]
    for r in range(ROWS):
        ocat[64 * r : 64 * (r + 1), :] = oc[:, r, :]
    ox_out[...] = ocat[...].T
    counted = [jnp.where(there, 1, 0) for there, _ in greet]
    pl.semaphore_wait(barrier, 1 + sum(counted))
    when(has_n, ocean_n.start)
    when(has_s, ocean_s.start)

    half_is0 = jnp.broadcast_to(me, (HALF, TILE)) == 0
    row_is0 = jnp.broadcast_to(me, (1, TILE)) == 0
    lane = lax.broadcasted_iota(jnp.int32, (HALF, TILE), 1)
    mine = jnp.where(lane < 64, 0, 1) == me
    mine_row = mine[:1]
    starts = [HALF + me * HALF + TILE * t for t in range(OWN)] + [other * (comps + HALF - 64)]
    spec_load.wait()
    for r in (3, 0, 1, 2):
        for t in range(OWN + 1):
            turned = spec[pl.ds(starts[t], TILE), r, :].T
            low, high = turned[:HALF], turned[HALF:]
            own = jnp.where(half_is0, low, high)
            state[t, r + 1, PAD : PAD + HALF] = own
            y_out[r, t] = jnp.where(half_is0, high, low).astype(b16)
            if r == 3:
                z1_out[0, t] = own.astype(b16)
            if r == 0:
                z1_out[1, t] = own.astype(b16)
            es_out[t, r : r + 1] = jnp.where(row_is0, turned[127:128], turned[0:1])
            ed_out[t, r : r + 1] = jnp.where(row_is0, turned[0:1], turned[127:128])
            ep_out[t, r : r + 1] = jnp.where(row_is0, turned[63:64], turned[64:65])
            el[t, r : r + 1] = jnp.where(row_is0, turned[64:65], turned[63:64])
        swap[r].start()
        if r == 3:
            when(has_n, z1_n.start)
        if r == 0:
            when(has_s, z1_s.start)
    when(has_same, e_same.start)
    when(has_far, e_diag.start)
    e_pair.start()
    when(has_e, ocean_e.start)
    when(has_w, ocean_w.start)

    wind_load.wait()
    mask_load.wait()
    table_load.wait()
    small[...] = jnp.zeros_like(small)
    small[0:4] = msk[...].astype(f32)
    small[4:8] = WIND_GAIN * wnd[0]
    small[8:12] = WIND_GAIN * wnd[1]
    small_t[...] = small[...].T
    columns = small_t[pl.ds(half_at, HALF), :]
    for q in range(3):
        for r in range(ROWS):
            n = 4 * q + r
            cells[2 + q, HALF * r : HALF * (r + 1), :] = jnp.broadcast_to(
                columns[:, n : n + 1], (HALF, TILE)
            )
    cb_load.wait()
    when(has_s, ocean_n.wait_recv)
    when(has_n, ocean_s.wait_recv)

    def choose(rows_ref, r, b, below, here, above):
        offset = jnp.broadcast_to(rows_ref[r, b, 0] - gy * ROWS - r, (1, COLS))
        return jnp.where(offset < 0, below, jnp.where(offset == 0, here, above))

    for k in range(2):
        at = 16 * k
        lines = [oz_in[0, at : at + 1]]
        lines += [oc[at : at + 1, r, :] for r in range(ROWS)]
        lines += [oz_in[1, at : at + 1]]
        for r in range(ROWS):
            total = cb[r, 0] * choose(crows, r, 0, *lines[r : r + 3])
            total = total + cb[r, 1] * choose(crows, r, 1, *lines[r : r + 3])
            cells[k, HALF * r : HALF * (r + 1), :] = jnp.broadcast_to(
                CURRENT_GAIN * total.sum(axis=1, keepdims=True), (HALF, TILE)
            )

    def edges(t, pair_side, far_side):
        for r in range(ROWS):
            near, far = pair_side[r : r + 1], far_side[r : r + 1]
            state[t, r + 1, PAD - 1 : PAD] = jnp.where(row_is0, far, near)
            state[t, r + 1, PAD + HALF : PAD + HALF + 1] = jnp.where(row_is0, near, far)

    def propagate(tiles, fresh, fresh_push):
        def body(r, carry):
            at = pl.multiple_of(r * HALF, HALF)
            for lo in (0, 32):
                cell = pl.ds(at + lo, 32)
                cur_x, cur_y, wet, wind_x, wind_y = (cells[q, cell, :] for q in range(5))
                zero = jnp.zeros((32, TILE), f32)
                totals = [
                    zero if (fresh if q < 2 else fresh_push) else sums[q, cell, :]
                    for q in range(4)
                ]
                for t in tiles:
                    speed_x, speed_y, cos, sin, phase, ratio = (
                        tab[t, q : q + 1, :] for q in range(6)
                    )
                    top = PAD + lo
                    here = state[t, r + 1, top : top + 32]
                    before = state[t, r + 1, top - 1 : top + 31]
                    after = state[t, r + 1, top + 1 : top + 33]
                    below = state[t, r, top : top + 32]
                    above = state[t, r + 2, top : top + 32]
                    cx = speed_x + cur_x
                    cy = speed_y + cur_y
                    flux = jnp.abs(cx) * (here - jnp.where(cx > 0.0, before, after))
                    flux = flux + jnp.abs(cy) * (here - jnp.where(cy > 0.0, below, above))
                    moved = wet * (here - flux)
                    growth = jnp.maximum(wind_x * cos + wind_y * sin - phase, 0.0)
                    pushed = growth * moved
                    prop[t, cell, :] = moved
                    rate[t, cell, :] = growth
                    p16[cell, TILE * t : TILE * (t + 1)] = moved.astype(b16)
                    parts = (moved, ratio * moved, pushed * cos, pushed * sin)
                    totals = [a + b for a, b in zip(totals, parts)]
                for q in range(4):
                    sums[q, cell, :] = totals[q]
            return carry

        lax.fori_loop(0, ROWS, body, 0)

    def finish_sums():
        total = STEPS * comps

        def spread(ref):
            return jnp.broadcast_to(ref.sum(axis=1, keepdims=True), (CELLS, TILE))

        floor = jnp.maximum(spread(sums[0]), 1.0)
        share = spread(sums[1]) / floor
        squared[...] = DECAY_GAIN * share * share
        gain[...] = (0.5 * total) / floor
        back[...] = (NONLINEAR_GAIN / total) * floor

    def dot(left, right):
        return lax.dot_general(
            left, right, (((1,), (0,)), ((), ())), preferred_element_type=f32
        )

    def activate(n, pre):
        for j in range(2):
            half = pre[:, TILE * j : TILE * (j + 1)] * gain[...]
            at = 256 * n + TILE * j
            hidden[:, at : at + TILE] = (half + half * jnp.tanh(half)).astype(b16)

    def update(tiles):
        at = TILE * tiles[0]
        moved = dot(hidden[...], w2[:, at : at + TILE * len(tiles)])
        for j, t in enumerate(tiles):
            transfer = moved[:, TILE * j : TILE * (j + 1)].astype(b16).astype(f32)
            fresh = prop[t] * jnp.exp(rate[t] - tab[t, 5:6, :] * squared[...])
            fresh = fresh + back[...] * transfer
            yield t, fresh

    when(has_s, z1_n.wait_recv)
    when(has_n, z1_s.wait_recv)
    when(has_far, e_same.wait_recv)
    for t in range(OWN):
        edges(t, el[t], es_in[t])
    for d, there in ((0, has_s), (1, has_n)):
        @pl.when(there)
        def _(d=d):
            for t in range(OWN):
                state[t, 5 * d, PAD : PAD + HALF] = z1_in[d, t].astype(f32)
    propagate(range(OWN), True, True)
    swap[3].wait_recv()
    when(has_n, zf_n.start)
    swap[0].wait_recv()
    when(has_s, zf_s.start)
    for copy in w1_loads:
        copy.wait()
    for n in range(4):
        lanes = slice(256 * n, 256 * (n + 1))
        part[:, lanes] = dot(p16[:, : TILE * OWN], w1[: TILE * OWN, lanes])

    when(has_w, ocean_e.wait_recv)
    when(has_e, ocean_w.wait_recv)
    from_w, from_e = ox_in[0].T, ox_in[1].T
    lane64 = lax.broadcasted_iota(jnp.int32, (64, COLS), 1)
    level64 = lax.rem(lax.broadcasted_iota(jnp.int32, (64, COLS), 0), 16)
    level = lax.broadcasted_iota(jnp.int32, (16, COLS), 0)

    def density(field):
        return HALINE * field[48:64] - THERMAL * field[32:48]

    def pressure(dense):
        running = dense
        for shift in (1, 2, 4, 8):
            running = running + jnp.where(level >= shift, pltpu.roll(running, shift, 0), 0.0)
        return running - 0.5 * dense

    for r in range(ROWS):
        here = oc[:, r, :]
        low = oz_in[0] if r == 0 else oc[:, r - 1, :]
        high = oz_in[1] if r == ROWS - 1 else oc[:, r + 1, :]
        lines = slice(64 * r, 64 * (r + 1))
        left = pltpu.roll(jnp.where(lane64 == COLS - 1, from_w[lines], here), 1, 1)
        right = pltpu.roll(jnp.where(lane64 == 0, from_e[lines], here), COLS - 1, 1)
        upper = jnp.where(level64 == 0, here, pltpu.roll(here, 1, 0))
        lower = jnp.where(level64 == 15, here, pltpu.roll(here, 63, 0))
        mixed = LATERAL_MIX * (left + right + low + high - 4.0 * here)
        mixed = mixed + VERTICAL_MIX * (upper + lower - 2.0 * here)
        across, along = right - left, high - low
        speed_u, speed_v = here[0:16], here[16:32]
        half_gain = 0.5 * PRESSURE_GAIN
        du = CORIOLIS * speed_v - half_gain * pressure(density(across))
        dv = -CORIOLIS * speed_u - half_gain * pressure(density(along))
        pull = -0.5 * ADVECTION
        dtemp = pull * (speed_u * across[32:48] + speed_v * along[32:48])
        dsalt = pull * (speed_u * across[48:64] + speed_v * along[48:64])
        tendency = mixed + jnp.concatenate([du, dv, dtemp, dsalt], axis=0)
        o_out[:, r, :] = here + msk[r : r + 1, :].astype(f32) * tendency

    swap[1].wait_recv()
    swap[2].wait_recv()
    for r in range(ROWS):
        for t in range(OWN):
            state[5 + t, r + 1, PAD : PAD + HALF] = y_in[r, t].astype(f32)
        state[4, r + 1, PAD : PAD + HALF] = jnp.where(
            mine, state[4, r + 1, PAD : PAD + HALF], y_in[r, 4].astype(f32)
        )
    when(has_far, e_diag.wait_recv)
    e_pair.wait_recv()
    for t in range(OWN):
        edges(5 + t, ep_in[t], ed_in[t])
    edges(4, jnp.where(mine[:8], el[4], ep_in[4]), jnp.where(mine[:8], es_in[4], ed_in[4]))
    for d, there, copy in ((0, has_s, zf_n), (1, has_n, zf_s)):
        @pl.when(there)
        def _(d=d, copy=copy):
            copy.wait_recv()
            for t in range(OWN):
                state[5 + t, 5 * d, PAD : PAD + HALF] = zf_in[d, t].astype(f32)
            state[4, 5 * d, PAD : PAD + HALF] = jnp.where(
                mine, z1_in[d, 4].astype(f32), zf_in[d, 4].astype(f32)
            )
    propagate(range(OWN, TILES), False, False)
    finish_sums()
    for n in range(4):
        lanes = slice(256 * n, 256 * (n + 1))
        activate(n, part[:, lanes] + dot(p16[:, TILE * OWN :], w1[TILE * OWN :, lanes]))
    for copy in w2_loads:
        copy.wait()
    for g, tiles in enumerate(GROUPS):
        for t, fresh in update(tiles):
            for r in range(ROWS):
                state[t, r + 1, PAD : PAD + HALF] = fresh[HALF * r : HALF * (r + 1)]
                begin, end = fresh[HALF * r : HALF * r + 1], fresh[HALF * r + 63 : HALF * r + 64]
                e2d_out[t, r : r + 1] = jnp.where(row_is0, begin, end)
                e2p_out[t, r : r + 1] = jnp.where(row_is0, end, begin)
            z2_out[0, t] = fresh[HALF * 3 :].astype(b16)
            z2_out[1, t] = fresh[:HALF].astype(b16)
        when(has_n, z2[g][0].start)
        when(has_s, z2[g][1].start)
        when(has_far, e2[g][0].start)
        e2[g][1].start()

    for g, tiles in enumerate(GROUPS):
        sender = SENDERS[g]
        when(has_far, e2[sender][0].wait_recv)
        e2[sender][1].wait_recv()
        for t in tiles:
            edges(t, e2p_in[t], e2d_in[t])
        for d, there in ((0, has_s), (1, has_n)):
            @pl.when(there)
            def _(d=d, g=g, tiles=tiles):
                z2[g][d].wait_recv()
                for t in tiles:
                    state[t, 5 * d, PAD : PAD + HALF] = z2_in[d, t].astype(f32)
        propagate(tiles, g == 0, False)
    finish_sums()
    scale = 1.0 / (STEPS * STEPS * comps)
    packed = jnp.zeros((HALF, TILE), f32)
    for k in range(2):
        for r in range(ROWS):
            push = sums[2 + k, HALF * r : HALF * (r + 1), :].sum(axis=1, keepdims=True)
            packed = jnp.where(lane == 4 * k + r, scale * push, packed)
    small[...] = jnp.zeros_like(small)
    small[pl.ds(half_at, HALF), :] = packed
    small_t[...] = small[...].T
    st_out[...] = small_t[0:8]
    stress_pair.start()
    for n in range(4):
        lanes = slice(256 * n, 256 * (n + 1))
        activate(n, dot(p16[...], w1[:, lanes]))
    stress_pair.wait_recv()
    st_full[...] = st_out[...] + st_in[...]
    when(has_n, stress_n.start)
    when(has_s, stress_s.start)
    for g, tiles in enumerate(LAST_GROUPS):
        for t, fresh in update(tiles):
            if t >= OWN:
                f_out[mirror(t)] = fresh.astype(b16)
            if t <= OWN:
                for r in range(ROWS):
                    state[t, r + 1, PAD : PAD + HALF] = fresh[HALF * r : HALF * (r + 1)]
        if g < 3:
            final[g].start()

    sb_load.wait()
    when(has_s, stress_n.wait_recv)
    when(has_n, stress_s.wait_recv)
    for k in range(2):
        lines = [sz_in[0, 4 * k + 3 : 4 * k + 4]]
        lines += [st_full[4 * k + r : 4 * k + r + 1] for r in range(ROWS)]
        lines += [sz_in[1, 4 * k : 4 * k + 1]]
        for r in range(ROWS):
            total = sb[r, 0] * choose(srows, r, 0, *lines[r : r + 3])
            total = total + sb[r, 1] * choose(srows, r, 1, *lines[r : r + 3])
            stress = total.T.sum(axis=0, keepdims=True)
            wet = msk[r : r + 1, :].astype(f32)
            at = 16 * k
            o_out[at : at + 1, r, :] = o_out[at : at + 1, r, :] + wet * (STRESS_GAIN * stress)

    for g in range(3):
        final[g].wait_recv()
        for t in ((0, 1), (2, 3), (4,))[g]:
            for r in range(ROWS):
                own = state[t, r + 1, PAD : PAD + HALF]
                came = f_in[t, HALF * r : HALF * (r + 1)].astype(f32)
                turned = jnp.concatenate(
                    [jnp.where(half_is0, own, came), jnp.where(half_is0, came, own)], axis=0
                ).T
                if t < OWN:
                    out[pl.ds(me * HALF + TILE * t, TILE), r, :] = turned
                else:
                    out[pl.ds(other * (comps - HALF), HALF), r, :] = jnp.where(
                        half_is0, turned[:HALF], turned[HALF:]
                    )

    when(has_n, ocean_n.wait_send, z1_n.wait_send, zf_n.wait_send, stress_n.wait_send)
    when(has_s, ocean_s.wait_send, z1_s.wait_send, zf_s.wait_send, stress_s.wait_send)
    when(has_e, ocean_e.wait_send)
    when(has_w, ocean_w.wait_send)
    when(has_same, e_same.wait_send)
    when(has_far, e_diag.wait_send)
    for copy in swap + [e_pair, stress_pair] + final:
        copy.wait_send()
    for g in range(len(GROUPS)):
        when(has_n, z2[g][0].wait_send)
        when(has_s, z2[g][1].wait_send)
        when(has_far, e2[g][0].wait_send)
        e2[g][1].wait_send()


def kernel_call(
    spectra, first, second, table, ocean, wind, mask, cblocks, sblocks, crows, srows
):
    f32, b16 = jnp.float32, jnp.bfloat16
    comps = spectra.shape[0]
    units = first.shape[1]
    total = TILE * TILES
    shape = jax.ShapeDtypeStruct
    dma = pltpu.SemaphoreType.DMA
    groups = len(GROUPS)
    vmem = pltpu.VMEM
    scratch = [
        vmem((comps + 2 * HALF, ROWS, COLS), f32),
        vmem((total, units), b16),
        vmem((units, total), b16),
        vmem((TILES, 8, TILE), f32),
        vmem(ocean.shape, f32),
        vmem(wind.shape, f32),
        vmem(mask.shape, jnp.int32),
        vmem((ROWS, 2, HALF, COLS), f32),
        vmem((ROWS, 2, COLS, COLS), f32),
        vmem((TILES, ROWS + 2, HALF + 2 * PAD, TILE), f32),
        vmem((TILES, CELLS, TILE), f32),
        vmem((TILES, CELLS, TILE), f32),
        vmem((CELLS, total), b16),
        vmem((CELLS, units), f32),
        vmem((CELLS, units), b16),
        vmem((4, CELLS, TILE), f32),
        vmem((5, CELLS, TILE), f32),
        vmem((CELLS, TILE), f32),
        vmem((CELLS, TILE), f32),
        vmem((CELLS, TILE), f32),
        vmem((TILE, TILE), f32),
        vmem((TILE, TILE), f32),
        vmem((ROWS, OWN + 1, HALF, TILE), b16),
        vmem((ROWS, OWN + 1, HALF, TILE), b16),
        vmem((2, OWN + 1, HALF, TILE), b16),
        vmem((2, OWN + 1, HALF, TILE), b16),
        vmem((2, OWN + 1, HALF, TILE), b16),
        *[vmem((OWN + 1, 8, TILE), f32) for _ in range(7)],
        vmem((2, TILES, HALF, TILE), b16),
        vmem((2, TILES, HALF, TILE), b16),
        *[vmem((TILES, 8, TILE), f32) for _ in range(4)],
        vmem((2, 64, COLS), f32),
        vmem((2, 64, COLS), f32),
        vmem((256, COLS), f32),
        vmem((COLS, 256), f32),
        vmem((2, COLS, 256), f32),
        vmem((8, COLS), f32),
        vmem((8, COLS), f32),
        vmem((8, COLS), f32),
        vmem((2, 8, COLS), f32),
        vmem((OWN + 1, CELLS, TILE), b16),
        vmem((OWN + 1, CELLS, TILE), b16),
        dma((13,)),
        dma((2,)), dma((2,)),
        dma((2,)), dma((2,)),
        dma((ROWS,)), dma((ROWS,)),
        dma((2,)), dma((2,)),
        dma((2,)), dma((2,)),
        dma((3,)), dma((3,)),
        dma((2, groups)), dma((2, groups)),
        dma((2, groups)), dma((2, groups)),
        dma((3,)), dma((3,)),
        dma((3,)), dma((3,)),
    ]
    return pl.pallas_call(
        kernel,
        out_shape=(shape(spectra.shape, f32), shape(ocean.shape, f32)),
        in_specs=[pl.BlockSpec(memory_space=pl.ANY)] * 9
        + [pl.BlockSpec(memory_space=pltpu.SMEM)] * 2,
        out_specs=(pl.BlockSpec(memory_space=pltpu.VMEM),) * 2,
        scratch_shapes=scratch,
        compiler_params=pltpu.CompilerParams(
            vmem_limit_bytes=VMEM_LIMIT, collective_id=0, has_side_effects=True
        ),
    )(spectra, first, second, table, ocean, wind, mask, cblocks, sblocks, crows, srows)


def local_step(
    spectra,
    wind_field,
    sea_mask,
    first_layer,
    second_layer,
    ocean_state,
    current_blocks,
    current_rows,
    stress_blocks,
    stress_rows,
):
    half_freqs, directions, rows, cols = spectra.shape
    variables, levels = ocean_state.shape[:2]
    table = jnp.asarray(tables(2 * half_freqs, directions))
    state, ocean = kernel_call(
        spectra.reshape(half_freqs * directions, rows, cols),
        first_layer,
        second_layer,
        table,
        ocean_state.reshape(variables * levels, rows, cols),
        wind_field,
        sea_mask,
        current_blocks,
        stress_blocks,
        current_rows,
        stress_rows,
    )
    return state.reshape(spectra.shape), ocean.reshape(ocean_state.shape)


def solution(mesh):
    placed = (
        P("comp", None, "gy", "gx"),
        P(None, "gy", "gx"),
        P("gy", "gx"),
        P(),
        P(),
        P(None, None, "gy", "gx"),
        P("gy", None, "gx", None),
        P("gy", None, "gx"),
        P("gy", None, "gx", None),
        P("gy", None, "gx"),
    )
    return jax.shard_map(
        local_step,
        mesh=mesh,
        in_specs=placed,
        out_specs=(P("comp", None, "gy", "gx"), P(None, None, "gy", "gx")),
        check_vma=False,
    )
```

profile of v0, /device:TPU:0, one launch (start us, length us, event | category | flops | bytes accessed | tf_op | source)
XLA Modules:
  0.0 41.2 jit_solution(18077641553517419073)
XLA Ops:
  0.6 1.4 %copy.13.crows = s32[4,2,1]{2,1,0:T(2,128)} copy(s32[4,2,1]{0,2,1:T(1,128)} %param.18) | data formatting | bytes 64 | tf_op args[7]
  2.0 1.4 %copy.14.srows = s32[4,2,1]{2,1,0:T(2,128)} copy(s32[4,2,1]{0,2,1:T(1,128)} %param.20) | data formatting | bytes 64 | tf_op args[9]
  3.3 34.8 %shard_map.122 = (f32[576,4,128]{2,1,0:T(4,128)}, f32[64,4,128]{2,1,0:T(4,128)}) custom-call(f32[576,4,128]{2,1,0:T(4,128)} %bitcast.4, bf16[1152,1024]{1,0:T(8,128)(2,1)} %first.1, bf16[1024,1152]{1,0:T(8,128)(2,1)} %second.1, f32[2,9,8,128]{3,2,1,0:T(8,128)} %constant.2.clone.table, f32[64,4,128]{2,1,0:T(4,128)} %bitcast.6, f32[2,4,128]{2,1,0:T(4,128)} %wind.1, ...), custom_call_target="tpu_custom_call" | custom-call | tf_op jit(solution)/shard_map/pallas_call | solution.py:612
  38.2 0.0 copy-start
  38.2 2.4 %copy.17 = f32[16,36,4,128]{3,2,1,0:T(4,128)} copy(f32[16,36,4,128]{3,2,1,0:T(4,128)} %bitcast.5) | data formatting | bytes 2359296
  40.6 0.0 copy-done
  40.6 0.7 %copy.18 = f32[4,16,4,128]{3,2,1,0:T(4,128)} copy(f32[4,16,4,128]{3,2,1,0:T(4,128)S(1)} %bitcast.7) | data formatting | bytes 262144
Async XLA Ops:
  38.2 2.4 %copy-start = (f32[64,4,128]{2,1,0:T(4,128)S(1)}, f32[64,4,128]{2,1,0:T(4,128)}, u32[]{:S(2)}) copy-start(f32[64,4,128]{2,1,0:T(4,128)} %get-tuple-element.5) | copy-start | bytes 393220
where the time goes:
time: 41.5 us; the launch traced here: 41.2 us
  Pallas kernels  34.8 us (84%)
  local copies, waits for them, and re-layouts  5.77 us (14%)
  between operations  0.65 us (2%)
    pallas_call x1, Pallas kernels, kernel_call(): pl.pallas_call(kernel, out_shape=(shape(spectra.shape, f32), shape(ocean....  34.8 us
    unnamed x6, local copies, waits for them, and re-layouts  5.77 us

commit v1 on v0

--- a/solution.py
+++ b/solution.py
@@ -31,8 +31,11 @@
 PAD = 8
 GROUPS = ((0, 1), (5, 6), (4,), (2, 3), (7, 8))
 SENDERS = (1, 0, 2, 4, 3)
-LAST_GROUPS = ((5, 6), (7, 8), (4,), (0, 1), (2, 3))
-VMEM_LIMIT = 56 * 1024 * 1024
+LAST_GROUPS = ((4,), (5, 6), (7, 8), (0, 1), (2, 3))
+ORDER = (1, 2, 0, 3)
+SWAPPED = ((3, 0), (1, 2))
+FINAL = (((0, 5), (5, 9)), ((0, 5), (5, 7), (7, 9)))
+VMEM_LIMIT = 32 * 1024 * 1024
 
 
 def tables(total, directions):
@@ -58,14 +61,14 @@
 
 
 def kernel(
-    spectra, first, second, table, ocean, wind, mask, cblocks, sblocks, crows, srows,
+    spectra, first, second, table, ocean, wind, mask, cblocks, sblocks, crows_in, srows_in,
     out, o_out,
     spec, w1, w2, tab, oc, wnd, msk, cb, sb,
     state, prop, rate, p16, part, hidden, sums, cells, gain, back, squared, small, small_t,
     y_out, y_in, z1_out, z1_in, zf_in, es_out, es_in, ed_out, ed_in, ep_out, ep_in, el,
     z2_out, z2_in, e2d_out, e2d_in, e2p_out, e2p_in,
-    oz_out, oz_in, ocat, ox_out, ox_in, st_out, st_in, st_full, sz_in, f_out, f_in,
-    load, oz_send, oz_recv, ox_send, ox_recv, y_send, y_recv, z1_send, z1_recv,
+    oz_out, oz_in, ocat, ox_out, ox_in, st_out, st_in, st_full, sz_in, f_out, f_in, done,
+    crows, srows, load, oz_send, oz_recv, ox_send, ox_recv, y_send, y_recv, z1_send, z1_recv,
     zf_send, zf_recv, e1_send, e1_recv, z2_send, z2_recv, e2_send, e2_recv,
     s_send, s_recv, f_send, f_recv,
 ):
@@ -100,9 +103,9 @@
         local(second.at[:, pl.ds(512, 128)], w2.at[:, pl.ds(512, 128)], 11),
         local(second.at[:, pl.ds(far_at, 512)], w2.at[:, pl.ds(640, 512)], 12),
     ]
-    all_loads = [ocean_load, spec_load, wind_load, mask_load, table_load, cb_load]
-    all_loads += w1_loads + w2_loads + [sb_load]
-    for copy in all_loads:
+    crows_load = local(crows_in, crows, 13)
+    srows_load = local(srows_in, srows, 14)
+    for copy in (spec_load, ocean_load, wind_load, mask_load, table_load, crows_load):
         copy.start()
 
     for ref in (es_in, ed_in, e2d_in, sz_in, ox_in, oz_in):
@@ -145,12 +148,18 @@
         ox_out.at[pl.ds(0, 8)], ox_in.at[1, pl.ds(0, 8)], ox_send.at[1], ox_recv.at[1], west
     )
     swap = [
-        remote(y_out.at[r], y_in.at[r], y_send.at[r], y_recv.at[r], pair) for r in range(ROWS)
+        [
+            remote(
+                y_out.at[p, part_of], y_in.at[p, part_of], y_send.at[p, n], y_recv.at[p, n], pair
+            )
+            for n, part_of in enumerate((pl.ds(0, 4), pl.ds(4, 5)))
+        ]
+        for p in range(2)
     ]
     z1_n = remote(z1_out.at[0], z1_in.at[0], z1_send.at[0], z1_recv.at[0], north)
     z1_s = remote(z1_out.at[1], z1_in.at[1], z1_send.at[1], z1_recv.at[1], south)
-    zf_n = remote(y_in.at[ROWS - 1], zf_in.at[0], zf_send.at[0], zf_recv.at[0], north)
-    zf_s = remote(y_in.at[0], zf_in.at[1], zf_send.at[1], zf_recv.at[1], south)
+    zf_n = remote(y_in.at[0, pl.ds(0, 5)], zf_in.at[0], zf_send.at[0], zf_recv.at[0], north)
+    zf_s = remote(y_in.at[0, pl.ds(4, 5)], zf_in.at[1], zf_send.at[1], zf_recv.at[1], south)
     e_same = remote(es_out, es_in, e1_send.at[0], e1_recv.at[0], same)
     e_diag = remote(ed_out, ed_in, e1_send.at[1], e1_recv.at[1], diag)
     e_pair = remote(ep_out, ep_in, e1_send.at[2], e1_recv.at[2], pair)
@@ -169,23 +178,24 @@
             )
             for d in range(2)
         ])
-        there = span(tuple(sorted(mirror(t) for t in tiles)))
+        there = SENDERS[g]
         e2.append([
-            remote(
-                e2d_out.at[part_of], e2d_in.at[there], e2_send.at[0, g], e2_recv.at[0, g], diag
-            ),
-            remote(
-                e2p_out.at[part_of], e2p_in.at[there], e2_send.at[1, g], e2_recv.at[1, g], pair
-            ),
+            remote(e2d_out.at[g], e2d_in.at[there], e2_send.at[0, g], e2_recv.at[0, g], diag),
+            remote(e2p_out.at[g], e2p_in.at[there], e2_send.at[1, g], e2_recv.at[1, g], pair),
         ])
     stress_pair = remote(st_out, st_in, s_send.at[0], s_recv.at[0], pair)
     stress_n = remote(st_full, sz_in.at[0], s_send.at[1], s_recv.at[1], north)
     stress_s = remote(st_full, sz_in.at[1], s_send.at[2], s_recv.at[2], south)
-    final_parts = (pl.ds(0, 2), pl.ds(2, 2), pl.ds(4, 1))
-    final = [
-        remote(f_out.at[p], f_in.at[p], f_send.at[n], f_recv.at[n], pair)
-        for n, p in enumerate(final_parts)
-    ]
+    final = []
+    for h in range(2):
+        final.append([])
+        for n, (begin, end) in enumerate(FINAL[h]):
+            slots = pl.ds(begin, end - begin)
+            final[h].append(
+                remote(
+                    f_out.at[h, slots], f_in.at[h, slots], f_send.at[h, n], f_recv.at[h, n], pair
+                )
+            )
 
     def when(condition, *actions):
         @pl.when(condition)
@@ -193,51 +203,78 @@
             for action in actions:
                 action()
 
-    state[...] = jnp.zeros_like(state)
+    for edge in (0, ROWS + 1):
+        state[:, edge, PAD : PAD + HALF] = jnp.zeros((TILES, HALF, TILE), f32)
     spec[:HALF] = jnp.zeros((HALF, ROWS, COLS), f32)
     spec[HALF + comps :] = jnp.zeros((HALF, ROWS, COLS), f32)
-
-    ocean_load.wait()
-    oz_out[0] = oc[:, ROWS - 1, :]
-    oz_out[1] = oc[:, 0, :]
-    for r in range(ROWS):
-        ocat[64 * r : 64 * (r + 1), :] = oc[:, r, :]
-    ox_out[...] = ocat[...].T
-    counted = [jnp.where(there, 1, 0) for there, _ in greet]
-    pl.semaphore_wait(barrier, 1 + sum(counted))
-    when(has_n, ocean_n.start)
-    when(has_s, ocean_s.start)
 
     half_is0 = jnp.broadcast_to(me, (HALF, TILE)) == 0
     row_is0 = jnp.broadcast_to(me, (1, TILE)) == 0
     lane = lax.broadcasted_iota(jnp.int32, (HALF, TILE), 1)
     mine = jnp.where(lane < 64, 0, 1) == me
-    mine_row = mine[:1]
+
+    def pack(first_row, second_row, low_lanes):
+        left = jnp.where(low_lanes, first_row, pltpu.roll(first_row, 64, 1))
+        right = jnp.where(low_lanes, pltpu.roll(second_row, 64, 1), second_row)
+        return jnp.where(lane < 64, left, right).astype(b16)
+
+    def unpack(packed, side, low_lanes):
+        wide = packed.astype(f32)
+        turned = pltpu.roll(wide, 64, 1)
+        if side == 0:
+            return jnp.where(low_lanes, wide, turned)
+        return jnp.where(low_lanes, turned, wide)
+
+    is_low, is_high = half_is0, jnp.logical_not(half_is0)
     starts = [HALF + me * HALF + TILE * t for t in range(OWN)] + [other * (comps + HALF - 64)]
     spec_load.wait()
-    for r in (3, 0, 1, 2):
-        for t in range(OWN + 1):
-            turned = spec[pl.ds(starts[t], TILE), r, :].T
-            low, high = turned[:HALF], turned[HALF:]
-            own = jnp.where(half_is0, low, high)
-            state[t, r + 1, PAD : PAD + HALF] = own
-            y_out[r, t] = jnp.where(half_is0, high, low).astype(b16)
+    for copy in [cb_load] + w1_loads + w2_loads + [sb_load, srows_load]:
+        copy.start()
+    counted = [jnp.where(there, 1, 0) for there, _ in greet]
+    for p, pair_rows in enumerate(SWAPPED):
+        kept = []
+        for side, r in enumerate(pair_rows):
+            for t in range(OWN + 1):
+                turned = spec[pl.ds(starts[t], TILE), r, :].T
+                low, high = turned[:HALF], turned[HALF:]
+                own = jnp.where(half_is0, low, high)
+                far = jnp.where(half_is0, high, low)
+                state[t, r + 1, PAD : PAD + HALF] = own
+                if t < OWN:
+                    y_out[p, 5 * side + t] = far.astype(b16)
+                else:
+                    kept.append(far)
+                if r == 3:
+                    z1_out[0, t] = own.astype(b16)
+                if r == 0:
+                    z1_out[1, t] = own.astype(b16)
+                at = 4 * t + r
+                es_out[at : at + 1] = jnp.where(row_is0, turned[127:128], turned[0:1])
+                ed_out[at : at + 1] = jnp.where(row_is0, turned[0:1], turned[127:128])
+                ep_out[at : at + 1] = jnp.where(row_is0, turned[63:64], turned[64:65])
+                el[at : at + 1] = jnp.where(row_is0, turned[64:65], turned[63:64])
             if r == 3:
-                z1_out[0, t] = own.astype(b16)
+                pl.semaphore_wait(barrier, 1 + sum(counted))
+            if side == 0:
+                swap[p][0].start()
+            if r == 3:
+                when(has_n, z1_n.start)
             if r == 0:
-                z1_out[1, t] = own.astype(b16)
-            es_out[t, r : r + 1] = jnp.where(row_is0, turned[127:128], turned[0:1])
-            ed_out[t, r : r + 1] = jnp.where(row_is0, turned[0:1], turned[127:128])
-            ep_out[t, r : r + 1] = jnp.where(row_is0, turned[63:64], turned[64:65])
-            el[t, r : r + 1] = jnp.where(row_is0, turned[64:65], turned[63:64])
-        swap[r].start()
-        if r == 3:
-            when(has_n, z1_n.start)
-        if r == 0:
-            when(has_s, z1_s.start)
+                when(has_s, z1_s.start)
+        y_out[p, 4] = pack(kept[0], kept[1], is_low)
+        swap[p][1].start()
     when(has_same, e_same.start)
     when(has_far, e_diag.start)
     e_pair.start()
+
+    ocean_load.wait()
+    oz_out[0] = oc[:, ROWS - 1, :]
+    oz_out[1] = oc[:, 0, :]
+    when(has_n, ocean_n.start)
+    when(has_s, ocean_s.start)
+    for r in range(ROWS):
+        ocat[64 * r : 64 * (r + 1), :] = oc[:, r, :]
+    ox_out[...] = ocat[...].T
     when(has_e, ocean_e.start)
     when(has_w, ocean_w.start)
 
@@ -253,15 +290,17 @@
     for q in range(3):
         for r in range(ROWS):
             n = 4 * q + r
-            cells[2 + q, HALF * r : HALF * (r + 1), :] = jnp.broadcast_to(
+            at = HALF * ORDER.index(r)
+            cells[2 + q, at : at + HALF, :] = jnp.broadcast_to(
                 columns[:, n : n + 1], (HALF, TILE)
             )
     cb_load.wait()
+    crows_load.wait()
     when(has_s, ocean_n.wait_recv)
     when(has_n, ocean_s.wait_recv)
 
     def choose(rows_ref, r, b, below, here, above):
-        offset = jnp.broadcast_to(rows_ref[r, b, 0] - gy * ROWS - r, (1, COLS))
+        offset = jnp.broadcast_to(rows_ref[b, 0, r] - gy * ROWS - r, (1, COLS))
         return jnp.where(offset < 0, below, jnp.where(offset == 0, here, above))
 
     for k in range(2):
@@ -272,7 +311,8 @@
         for r in range(ROWS):
             total = cb[r, 0] * choose(crows, r, 0, *lines[r : r + 3])
             total = total + cb[r, 1] * choose(crows, r, 1, *lines[r : r + 3])
-            cells[k, HALF * r : HALF * (r + 1), :] = jnp.broadcast_to(
+            place = HALF * ORDER.index(r)
+            cells[k, place : place + HALF, :] = jnp.broadcast_to(
                 CURRENT_GAIN * total.sum(axis=1, keepdims=True), (HALF, TILE)
             )
 
@@ -282,9 +322,10 @@
             state[t, r + 1, PAD - 1 : PAD] = jnp.where(row_is0, far, near)
             state[t, r + 1, PAD + HALF : PAD + HALF + 1] = jnp.where(row_is0, near, far)
 
-    def propagate(tiles, fresh, fresh_push):
-        def body(r, carry):
-            at = pl.multiple_of(r * HALF, HALF)
+    def propagate(tiles, h, fresh, fresh_push):
+        def body(i, carry):
+            at = pl.multiple_of((2 * h + i) * HALF, HALF)
+            r = 3 * i if h else 1 + i
             for lo in (0, 32):
                 cell = pl.ds(at + lo, 32)
                 cur_x, cur_y, wet, wind_x, wind_y = (cells[q, cell, :] for q in range(5))
@@ -319,54 +360,60 @@
                     sums[q, cell, :] = totals[q]
             return carry
 
-        lax.fori_loop(0, ROWS, body, 0)
-
-    def finish_sums():
+        lax.fori_loop(0, 2, body, 0)
+
+    def finish_sums(rows):
         total = STEPS * comps
-
-        def spread(ref):
-            return jnp.broadcast_to(ref.sum(axis=1, keepdims=True), (CELLS, TILE))
-
-        floor = jnp.maximum(spread(sums[0]), 1.0)
-        share = spread(sums[1]) / floor
-        squared[...] = DECAY_GAIN * share * share
-        gain[...] = (0.5 * total) / floor
-        back[...] = (NONLINEAR_GAIN / total) * floor
+        count = rows.stop - rows.start
+
+        def spread(n):
+            return jnp.broadcast_to(
+                sums[n, rows, :].sum(axis=1, keepdims=True), (count, TILE)
+            )
+
+        floor = jnp.maximum(spread(0), 1.0)
+        share = spread(1) / floor
+        squared[rows] = DECAY_GAIN * share * share
+        gain[rows] = (0.5 * total) / floor
+        back[rows] = (NONLINEAR_GAIN / total) * floor
 
     def dot(left, right):
         return lax.dot_general(
             left, right, (((1,), (0,)), ((), ())), preferred_element_type=f32
         )
 
-    def activate(n, pre):
+    def activate(n, pre, rows):
         for j in range(2):
-            half = pre[:, TILE * j : TILE * (j + 1)] * gain[...]
+            half = pre[:, TILE * j : TILE * (j + 1)] * gain[rows]
             at = 256 * n + TILE * j
-            hidden[:, at : at + TILE] = (half + half * jnp.tanh(half)).astype(b16)
-
-    def update(tiles):
+            hidden[rows, at : at + TILE] = (half + half * jnp.tanh(half)).astype(b16)
+
+    def update(tiles, rows):
         at = TILE * tiles[0]
-        moved = dot(hidden[...], w2[:, at : at + TILE * len(tiles)])
+        moved = dot(hidden[rows], w2[:, at : at + TILE * len(tiles)])
         for j, t in enumerate(tiles):
             transfer = moved[:, TILE * j : TILE * (j + 1)].astype(b16).astype(f32)
-            fresh = prop[t] * jnp.exp(rate[t] - tab[t, 5:6, :] * squared[...])
-            fresh = fresh + back[...] * transfer
-            yield t, fresh
+            fresh = prop[t, rows] * jnp.exp(rate[t, rows] - tab[t, 5:6, :] * squared[rows])
+            yield j, t, fresh + back[rows] * transfer
+
+    whole = slice(0, CELLS)
+    halves = (slice(0, CELLS // 2), slice(CELLS // 2, CELLS))
 
     when(has_s, z1_n.wait_recv)
     when(has_n, z1_s.wait_recv)
     when(has_far, e_same.wait_recv)
     for t in range(OWN):
-        edges(t, el[t], es_in[t])
+        edges(t, el[4 * t : 4 * t + 4], es_in[4 * t : 4 * t + 4])
     for d, there in ((0, has_s), (1, has_n)):
         @pl.when(there)
         def _(d=d):
             for t in range(OWN):
                 state[t, 5 * d, PAD : PAD + HALF] = z1_in[d, t].astype(f32)
-    propagate(range(OWN), True, True)
-    swap[3].wait_recv()
+    for h in range(2):
+        propagate(range(OWN), h, True, True)
+    swap[0][0].wait_recv()
+    swap[0][1].wait_recv()
     when(has_n, zf_n.start)
-    swap[0].wait_recv()
     when(has_s, zf_s.start)
     for copy in w1_loads:
         copy.wait()
@@ -412,68 +459,108 @@
         tendency = mixed + jnp.concatenate([du, dv, dtemp, dsalt], axis=0)
         o_out[:, r, :] = here + msk[r : r + 1, :].astype(f32) * tendency
 
-    swap[1].wait_recv()
-    swap[2].wait_recv()
-    for r in range(ROWS):
-        for t in range(OWN):
-            state[5 + t, r + 1, PAD : PAD + HALF] = y_in[r, t].astype(f32)
-        state[4, r + 1, PAD : PAD + HALF] = jnp.where(
-            mine, state[4, r + 1, PAD : PAD + HALF], y_in[r, 4].astype(f32)
-        )
+    for p, pair_rows in enumerate(SWAPPED):
+        if p == 1:
+            swap[1][0].wait_recv()
+            swap[1][1].wait_recv()
+        for side, r in enumerate(pair_rows):
+            for t in range(OWN):
+                state[5 + t, r + 1, PAD : PAD + HALF] = y_in[p, 5 * side + t].astype(f32)
+            state[4, r + 1, PAD : PAD + HALF] = jnp.where(
+                mine, state[4, r + 1, PAD : PAD + HALF], unpack(y_in[p, 4], side, is_high)
+            )
     when(has_far, e_diag.wait_recv)
     e_pair.wait_recv()
     for t in range(OWN):
-        edges(5 + t, ep_in[t], ed_in[t])
-    edges(4, jnp.where(mine[:8], el[4], ep_in[4]), jnp.where(mine[:8], es_in[4], ed_in[4]))
+        lines = slice(4 * t, 4 * t + 4)
+        edges(5 + t, ep_in[lines], ed_in[lines])
+    edges(
+        4,
+        jnp.where(mine[:4], el[16:20], ep_in[16:20]),
+        jnp.where(mine[:4], es_in[16:20], ed_in[16:20]),
+    )
     for d, there, copy in ((0, has_s, zf_n), (1, has_n, zf_s)):
         @pl.when(there)
         def _(d=d, copy=copy):
             copy.wait_recv()
             for t in range(OWN):
-                state[5 + t, 5 * d, PAD : PAD + HALF] = zf_in[d, t].astype(f32)
+                state[5 + t, 5 * d, PAD : PAD + HALF] = zf_in[d, t + d].astype(f32)
             state[4, 5 * d, PAD : PAD + HALF] = jnp.where(
-                mine, z1_in[d, 4].astype(f32), zf_in[d, 4].astype(f32)
+                mine, z1_in[d, 4].astype(f32), unpack(zf_in[d, 4 - 4 * d], d, is_high)
             )
-    propagate(range(OWN, TILES), False, False)
-    finish_sums()
+    for h in range(2):
+        propagate(range(OWN, TILES), h, False, False)
+    finish_sums(whole)
     for n in range(4):
         lanes = slice(256 * n, 256 * (n + 1))
-        activate(n, part[:, lanes] + dot(p16[:, TILE * OWN :], w1[TILE * OWN :, lanes]))
+        pre = part[:, lanes] + dot(p16[:, TILE * OWN :], w1[TILE * OWN :, lanes])
+        activate(n, pre, whole)
     for copy in w2_loads:
         copy.wait()
     for g, tiles in enumerate(GROUPS):
-        for t, fresh in update(tiles):
-            for r in range(ROWS):
-                state[t, r + 1, PAD : PAD + HALF] = fresh[HALF * r : HALF * (r + 1)]
-                begin, end = fresh[HALF * r : HALF * r + 1], fresh[HALF * r + 63 : HALF * r + 64]
-                e2d_out[t, r : r + 1] = jnp.where(row_is0, begin, end)
-                e2p_out[t, r : r + 1] = jnp.where(row_is0, end, begin)
-            z2_out[0, t] = fresh[HALF * 3 :].astype(b16)
-            z2_out[1, t] = fresh[:HALF].astype(b16)
+        for j, t, fresh in update(tiles, whole):
+            for n, r in enumerate(ORDER):
+                block = fresh[HALF * n : HALF * (n + 1)]
+                state[t, r + 1, PAD : PAD + HALF] = block
+                begin, end = block[:1], block[HALF - 1 :]
+                at = 4 * j + r
+                e2d_out[g, at : at + 1] = jnp.where(row_is0, begin, end)
+                e2p_out[g, at : at + 1] = jnp.where(row_is0, end, begin)
+                if r == ROWS - 1:
+                    z2_out[0, t] = block.astype(b16)
+                if r == 0:
+                    z2_out[1, t] = block.astype(b16)
+        when(has_far, e2[g][0].start)
+        e2[g][1].start()
         when(has_n, z2[g][0].start)
         when(has_s, z2[g][1].start)
-        when(has_far, e2[g][0].start)
-        e2[g][1].start()
+
+    def last_updates(h):
+        rows = halves[h]
+        for tiles in LAST_GROUPS:
+            for j, t, fresh in update(tiles, rows):
+                upper, under = fresh[:HALF], fresh[HALF:]
+                if t > OWN:
+                    at = 1 + 2 * (t - 5)
+                    f_out[h, at] = upper.astype(b16)
+                    f_out[h, at + 1] = under.astype(b16)
+                if t == OWN:
+                    f_out[h, 0] = pack(upper, under, is_high)
+                if t <= OWN:
+                    done[t, rows] = fresh
+            if tiles == (5, 6):
+                final[h][0].start()
+            if tiles == (7, 8):
+                for copy in final[h][1:]:
+                    copy.start()
 
     for g, tiles in enumerate(GROUPS):
-        sender = SENDERS[g]
-        when(has_far, e2[sender][0].wait_recv)
-        e2[sender][1].wait_recv()
-        for t in tiles:
-            edges(t, e2p_in[t], e2d_in[t])
+        when(has_far, e2[SENDERS[g]][0].wait_recv)
+        e2[SENDERS[g]][1].wait_recv()
+        for j, t in enumerate(tiles):
+            lines = slice(4 * j, 4 * j + 4)
+            edges(t, e2p_in[g, lines], e2d_in[g, lines])
+        propagate(tiles, 0, g == 0, False)
+    finish_sums(halves[0])
+    for n in range(4):
+        lanes = slice(256 * n, 256 * (n + 1))
+        activate(n, dot(p16[halves[0]], w1[:, lanes]), halves[0])
+    last_updates(0)
+
+    for g, tiles in enumerate(GROUPS):
         for d, there in ((0, has_s), (1, has_n)):
             @pl.when(there)
             def _(d=d, g=g, tiles=tiles):
                 z2[g][d].wait_recv()
                 for t in tiles:
                     state[t, 5 * d, PAD : PAD + HALF] = z2_in[d, t].astype(f32)
-        propagate(tiles, g == 0, False)
-    finish_sums()
+        propagate(tiles, 1, g == 0, False)
+    finish_sums(halves[1])
     scale = 1.0 / (STEPS * STEPS * comps)
     packed = jnp.zeros((HALF, TILE), f32)
     for k in range(2):
-        for r in range(ROWS):
-            push = sums[2 + k, HALF * r : HALF * (r + 1), :].sum(axis=1, keepdims=True)
+        for n, r in enumerate(ORDER):
+            push = sums[2 + k, HALF * n : HALF * (n + 1), :].sum(axis=1, keepdims=True)
             packed = jnp.where(lane == 4 * k + r, scale * push, packed)
     small[...] = jnp.zeros_like(small)
     small[pl.ds(half_at, HALF), :] = packed
@@ -482,22 +569,41 @@
     stress_pair.start()
     for n in range(4):
         lanes = slice(256 * n, 256 * (n + 1))
-        activate(n, dot(p16[...], w1[:, lanes]))
+        activate(n, dot(p16[halves[1]], w1[:, lanes]), halves[1])
+    last_updates(1)
     stress_pair.wait_recv()
     st_full[...] = st_out[...] + st_in[...]
     when(has_n, stress_n.start)
     when(has_s, stress_s.start)
-    for g, tiles in enumerate(LAST_GROUPS):
-        for t, fresh in update(tiles):
-            if t >= OWN:
-                f_out[mirror(t)] = fresh.astype(b16)
-            if t <= OWN:
-                for r in range(ROWS):
-                    state[t, r + 1, PAD : PAD + HALF] = fresh[HALF * r : HALF * (r + 1)]
-        if g < 3:
-            final[g].start()
+
+    def turn_back(h, t):
+        for side in range(2):
+            n = 2 * h + side
+            own = done[t, HALF * n : HALF * (n + 1)]
+            if t < OWN:
+                came = f_in[h, 1 + 2 * t + side].astype(f32)
+            else:
+                came = unpack(f_in[h, 0], side, is_low)
+            turned = jnp.concatenate(
+                [jnp.where(half_is0, own, came), jnp.where(half_is0, came, own)], axis=0
+            ).T
+            r = ORDER[n]
+            if t < OWN:
+                out[pl.ds(me * HALF + TILE * t, TILE), r, :] = turned
+            else:
+                out[pl.ds(other * (comps - HALF), HALF), r, :] = jnp.where(
+                    half_is0, turned[:HALF], turned[HALF:]
+                )
+
+    final[0][0].wait_recv()
+    for t in (4, 0, 1):
+        turn_back(0, t)
+    final[0][1].wait_recv()
+    for t in (2, 3):
+        turn_back(0, t)
 
     sb_load.wait()
+    srows_load.wait()
     when(has_s, stress_n.wait_recv)
     when(has_n, stress_s.wait_recv)
     for k in range(2):
@@ -512,21 +618,10 @@
             at = 16 * k
             o_out[at : at + 1, r, :] = o_out[at : at + 1, r, :] + wet * (STRESS_GAIN * stress)
 
-    for g in range(3):
-        final[g].wait_recv()
-        for t in ((0, 1), (2, 3), (4,))[g]:
-            for r in range(ROWS):
-                own = state[t, r + 1, PAD : PAD + HALF]
-                came = f_in[t, HALF * r : HALF * (r + 1)].astype(f32)
-                turned = jnp.concatenate(
-                    [jnp.where(half_is0, own, came), jnp.where(half_is0, came, own)], axis=0
-                ).T
-                if t < OWN:
-                    out[pl.ds(me * HALF + TILE * t, TILE), r, :] = turned
-                else:
-                    out[pl.ds(other * (comps - HALF), HALF), r, :] = jnp.where(
-                        half_is0, turned[:HALF], turned[HALF:]
-                    )
+    for n, tiles in enumerate(((4, 0, 1), (2,), (3,))):
+        final[1][n].wait_recv()
+        for t in tiles:
+            turn_back(1, t)
 
     when(has_n, ocean_n.wait_send, z1_n.wait_send, zf_n.wait_send, stress_n.wait_send)
     when(has_s, ocean_s.wait_send, z1_s.wait_send, zf_s.wait_send, stress_s.wait_send)
@@ -534,7 +629,7 @@
     when(has_w, ocean_w.wait_send)
     when(has_same, e_same.wait_send)
     when(has_far, e_diag.wait_send)
-    for copy in swap + [e_pair, stress_pair] + final:
+    for copy in swap[0] + swap[1] + [e_pair, stress_pair] + final[0] + final[1]:
         copy.wait_send()
     for g in range(len(GROUPS)):
         when(has_n, z2[g][0].wait_send)
@@ -577,15 +672,15 @@
         vmem((CELLS, TILE), f32),
         vmem((TILE, TILE), f32),
         vmem((TILE, TILE), f32),
-        vmem((ROWS, OWN + 1, HALF, TILE), b16),
-        vmem((ROWS, OWN + 1, HALF, TILE), b16),
+        vmem((2, TILES, HALF, TILE), b16),
+        vmem((2, TILES, HALF, TILE), b16),
         vmem((2, OWN + 1, HALF, TILE), b16),
         vmem((2, OWN + 1, HALF, TILE), b16),
         vmem((2, OWN + 1, HALF, TILE), b16),
-        *[vmem((OWN + 1, 8, TILE), f32) for _ in range(7)],
+        *[vmem((24, TILE), f32) for _ in range(7)],
         vmem((2, TILES, HALF, TILE), b16),
         vmem((2, TILES, HALF, TILE), b16),
-        *[vmem((TILES, 8, TILE), f32) for _ in range(4)],
+        *[vmem((groups, 8, TILE), f32) for _ in range(4)],
         vmem((2, 64, COLS), f32),
         vmem((2, 64, COLS), f32),
         vmem((256, COLS), f32),
@@ -595,31 +690,65 @@
         vmem((8, COLS), f32),
         vmem((8, COLS), f32),
         vmem((2, 8, COLS), f32),
-        vmem((OWN + 1, CELLS, TILE), b16),
-        vmem((OWN + 1, CELLS, TILE), b16),
-        dma((13,)),
+        vmem((2, TILES, HALF, TILE), b16),
+        vmem((2, TILES, HALF, TILE), b16),
+        vmem((OWN + 1, CELLS, TILE), f32),
+        pltpu.SMEM((2, 1, ROWS), jnp.int32),
+        pltpu.SMEM((2, 1, ROWS), jnp.int32),
+        dma((15,)),
         dma((2,)), dma((2,)),
         dma((2,)), dma((2,)),
-        dma((ROWS,)), dma((ROWS,)),
+        dma((2, 2)), dma((2, 2)),
         dma((2,)), dma((2,)),
         dma((2,)), dma((2,)),
         dma((3,)), dma((3,)),
         dma((2, groups)), dma((2, groups)),
         dma((2, groups)), dma((2, groups)),
         dma((3,)), dma((3,)),
-        dma((3,)), dma((3,)),
+        dma((2, 3)), dma((2, 3)),
     ]
     return pl.pallas_call(
         kernel,
         out_shape=(shape(spectra.shape, f32), shape(ocean.shape, f32)),
-        in_specs=[pl.BlockSpec(memory_space=pl.ANY)] * 9
-        + [pl.BlockSpec(memory_space=pltpu.SMEM)] * 2,
+        in_specs=[pl.BlockSpec(memory_space=pl.ANY)] * 11,
         out_specs=(pl.BlockSpec(memory_space=pltpu.VMEM),) * 2,
         scratch_shapes=scratch,
         compiler_params=pltpu.CompilerParams(
             vmem_limit_bytes=VMEM_LIMIT, collective_id=0, has_side_effects=True
         ),
-    )(spectra, first, second, table, ocean, wind, mask, cblocks, sblocks, crows, srows)
+    )(*(
+        pltpu.with_memory_space_constraint(x, pltpu.HBM)
+        for x in (
+            spectra, first, second, table, ocean, wind, mask, cblocks, sblocks, crows, srows
+        )
+    ))
+
+
+PIECES = 4
+
+
+def place_kernel(a, b, a_out, b_out, sems):
+    rows = a.shape[0] // PIECES
+    copies = [pltpu.make_async_copy(b, b_out, sems.at[PIECES])]
+    for n in range(PIECES):
+        part = pl.ds(n * rows, rows)
+        copies.append(pltpu.make_async_copy(a.at[part], a_out.at[part], sems.at[n]))
+    for copy in copies:
+        copy.start()
+    for copy in copies:
+        copy.wait()
+
+
+def place_call(a, b):
+    shape = jax.ShapeDtypeStruct
+    return pl.pallas_call(
+        place_kernel,
+        out_shape=(shape(a.shape, a.dtype), shape(b.shape, b.dtype)),
+        in_specs=[pl.BlockSpec(memory_space=pl.ANY)] * 2,
+        out_specs=(pl.BlockSpec(memory_space=pl.ANY),) * 2,
+        scratch_shapes=[pltpu.SemaphoreType.DMA((PIECES + 1,))],
+        compiler_params=pltpu.CompilerParams(vmem_limit_bytes=VMEM_LIMIT),
+    )(a, b)
 
 
 def local_step(
@@ -647,9 +776,10 @@
         sea_mask,
         current_blocks,
         stress_blocks,
-        current_rows,
-        stress_rows,
+        current_rows.transpose(1, 2, 0),
+        stress_rows.transpose(1, 2, 0),
     )
+    state, ocean = place_call(state, ocean)
     return state.reshape(spectra.shape), ocean.reshape(ocean_state.shape)
 
 

time: 41.5 us -> 32.8 us (0.79)
  local copies, waits for them, and re-layouts: 5.77 us -> 0 us
  Pallas kernels: 34.8 us -> 32 us
    unnamed x6 -> x0, local copies, waits for them, and re-layouts: 5.77 us -> none
    pallas_call x1, Pallas kernels: 34.8 us -> 30.9 us  [kernel_call(): pl.pallas_call(kernel, out_shape=(shape(spectra.shape, f32), shape(ocean....]
    pallas_call x0 -> x1, Pallas kernels: none -> 1.09 us  [place_call(): pl.pallas_call(place_kernel, out_shape=(shape(a.shape, a.dtype), shape(b....]
where the time goes in v1:
time: 32.8 us; the launch traced here: 32.7 us
  Pallas kernels  32 us (98%)
  between operations  0.64 us (2%)
    pallas_call x1, Pallas kernels, kernel_call(): pl.pallas_call(kernel, out_shape=(shape(spectra.shape, f32), shape(ocean....  30.9 us
    pallas_call x1, Pallas kernels, place_call(): pl.pallas_call(place_kernel, out_shape=(shape(a.shape, a.dtype), shape(b....  1.09 us

profile of v1, /device:TPU:0, one launch (start us, length us, event | category | flops | bytes accessed | tf_op | source)
XLA Modules:
  0.0 32.7 jit_solution(7318607605383769020)
XLA Ops:
  0.6 30.9 %shard_map.122 = (f32[576,4,128]{2,1,0:T(4,128)S(1)}, f32[64,4,128]{2,1,0:T(4,128)S(1)}) custom-call(f32[576,4,128]{2,1,0:T(4,128)} %bitcast.6, bf16[1152,1024]{1,0:T(8,128)(2,1)} %first.1, bf16[1024,1152]{1,0:T(8,128)(2,1)} %second.1, f32[2,9,8,128]{3,2,1,0:T(8,128)} %constant.2.clone.table, f32[64,4,128]{2,1,0:T(4,128)} %bitcast.7, f32[2,4,128]{2,1,0:T(4,128)} %wind.1, ...), custom_call_target="tpu_custom_call" | custom-call | tf_op jit(solution)/shard_map/pallas_call | solution.py:710
  31.6 1.1 %shard_map.123 = (f32[576,4,128]{2,1,0:T(4,128)}, f32[64,4,128]{2,1,0:T(4,128)}) custom-call(f32[576,4,128]{2,1,0:T(4,128)S(1)} %get-tuple-element.6.a, f32[64,4,128]{2,1,0:T(4,128)S(1)} %get-tuple-element.7.b), custom_call_target="tpu_custom_call" | custom-call | tf_op jit(solution)/shard_map/pallas_call | solution.py:744

commit v2 on v1

--- a/solution.py
+++ b/solution.py
@@ -29,12 +29,18 @@
 TILES = 9
 OWN = 4
 PAD = 8
-GROUPS = ((0, 1), (5, 6), (4,), (2, 3), (7, 8))
-SENDERS = (1, 0, 2, 4, 3)
-LAST_GROUPS = ((4,), (5, 6), (7, 8), (0, 1), (2, 3))
+GROUPS = ((0, 1, 5, 6), (2, 3, 7, 8, 4))
+PLACED = GROUPS[0] + GROUPS[1]
+PRODUCTS = (((0, 1), (5, 6)), ((2, 3), (7, 8), (4,)))
+SWAP_SLOTS = (
+    (pl.ds(0, 2), pl.ds(7, 2), pl.ds(2, 3), pl.ds(5, 2)),
+    (pl.ds(0, 5), pl.ds(5, 4)),
+)
+NORTH_SLOTS = ((pl.ds(0, 2), pl.ds(0, 2)), (pl.ds(2, 3), pl.ds(2, 3)))
+SOUTH_SLOTS = ((pl.ds(7, 2), pl.ds(3, 2)), (pl.ds(4, 3), pl.ds(0, 3)))
 ORDER = (1, 2, 0, 3)
 SWAPPED = ((3, 0), (1, 2))
-FINAL = (((0, 5), (5, 9)), ((0, 5), (5, 7), (7, 9)))
+FINAL = (((0, 4), (4, 9)), ((0, 4), (4, 8), (8, 9)))
 VMEM_LIMIT = 32 * 1024 * 1024
 
 
@@ -67,7 +73,7 @@
     state, prop, rate, p16, part, hidden, sums, cells, gain, back, squared, small, small_t,
     y_out, y_in, z1_out, z1_in, zf_in, es_out, es_in, ed_out, ed_in, ep_out, ep_in, el,
     z2_out, z2_in, e2d_out, e2d_in, e2p_out, e2p_in,
-    oz_out, oz_in, ocat, ox_out, ox_in, st_out, st_in, st_full, sz_in, f_out, f_in, done,
+    oz_out, oz_in, ocat, ox_out, ox_in, st_out, st_in, st_full, sz_in, sx_in, f_out, f_in, done,
     crows, srows, load, oz_send, oz_recv, ox_send, ox_recv, y_send, y_recv, z1_send, z1_recv,
     zf_send, zf_recv, e1_send, e1_recv, z2_send, z2_recv, e2_send, e2_recv,
     s_send, s_recv, f_send, f_recv,
@@ -108,7 +114,7 @@
     for copy in (spec_load, ocean_load, wind_load, mask_load, table_load, crows_load):
         copy.start()
 
-    for ref in (es_in, ed_in, e2d_in, sz_in, ox_in, oz_in):
+    for ref in (es_in, ed_in, e2d_in, sz_in, sx_in, ox_in, oz_in):
         ref[...] = jnp.zeros_like(ref)
 
     has_s, has_n = gy > 0, gy < ny - 1
@@ -127,6 +133,8 @@
 
     barrier = pltpu.get_barrier_semaphore()
     greet = ((has_s, south), (has_n, north), (has_w, west), (has_e, east), (has_far, diag))
+    other_n, other_s = {**pair, **north}, {**pair, **south}
+    greet += ((has_n, other_n), (has_s, other_s))
     for there, place in greet:
         @pl.when(there)
         def _(place=place):
@@ -152,25 +160,28 @@
             remote(
                 y_out.at[p, part_of], y_in.at[p, part_of], y_send.at[p, n], y_recv.at[p, n], pair
             )
-            for n, part_of in enumerate((pl.ds(0, 4), pl.ds(4, 5)))
+            for n, part_of in enumerate(SWAP_SLOTS[p])
         ]
         for p in range(2)
     ]
     z1_n = remote(z1_out.at[0], z1_in.at[0], z1_send.at[0], z1_recv.at[0], north)
     z1_s = remote(z1_out.at[1], z1_in.at[1], z1_send.at[1], z1_recv.at[1], south)
-    zf_n = remote(y_in.at[0, pl.ds(0, 5)], zf_in.at[0], zf_send.at[0], zf_recv.at[0], north)
-    zf_s = remote(y_in.at[0, pl.ds(4, 5)], zf_in.at[1], zf_send.at[1], zf_recv.at[1], south)
+    zf_n = [
+        remote(y_in.at[0, a], zf_in.at[0, b], zf_send.at[0, n], zf_recv.at[0, n], north)
+        for n, (a, b) in enumerate(NORTH_SLOTS)
+    ]
+    zf_s = [
+        remote(y_in.at[0, a], zf_in.at[1, b], zf_send.at[1, n], zf_recv.at[1, n], south)
+        for n, (a, b) in enumerate(SOUTH_SLOTS)
+    ]
     e_same = remote(es_out, es_in, e1_send.at[0], e1_recv.at[0], same)
     e_diag = remote(ed_out, ed_in, e1_send.at[1], e1_recv.at[1], diag)
     e_pair = remote(ep_out, ep_in, e1_send.at[2], e1_recv.at[2], pair)
 
-    def span(tiles):
-        return pl.ds(tiles[0], len(tiles))
-
     z2 = []
     e2 = []
     for g, tiles in enumerate(GROUPS):
-        part_of = span(tiles)
+        part_of = pl.ds(PLACED.index(tiles[0]), len(tiles))
         z2.append([
             remote(
                 z2_out.at[d, part_of], z2_in.at[d, part_of],
@@ -178,14 +189,15 @@
             )
             for d in range(2)
         ])
-        there = SENDERS[g]
         e2.append([
-            remote(e2d_out.at[g], e2d_in.at[there], e2_send.at[0, g], e2_recv.at[0, g], diag),
-            remote(e2p_out.at[g], e2p_in.at[there], e2_send.at[1, g], e2_recv.at[1, g], pair),
+            remote(e2d_out.at[g], e2d_in.at[g], e2_send.at[0, g], e2_recv.at[0, g], diag),
+            remote(e2p_out.at[g], e2p_in.at[g], e2_send.at[1, g], e2_recv.at[1, g], pair),
         ])
     stress_pair = remote(st_out, st_in, s_send.at[0], s_recv.at[0], pair)
-    stress_n = remote(st_full, sz_in.at[0], s_send.at[1], s_recv.at[1], north)
-    stress_s = remote(st_full, sz_in.at[1], s_send.at[2], s_recv.at[2], south)
+    stress_n = remote(st_out, sz_in.at[0], s_send.at[1], s_recv.at[1], north)
+    stress_s = remote(st_out, sz_in.at[1], s_send.at[2], s_recv.at[2], south)
+    stress_on = remote(st_out, sx_in.at[0], s_send.at[3], s_recv.at[3], other_n)
+    stress_os = remote(st_out, sx_in.at[1], s_send.at[4], s_recv.at[4], other_s)
     final = []
     for h in range(2):
         final.append([])
@@ -231,41 +243,55 @@
     for copy in [cb_load] + w1_loads + w2_loads + [sb_load, srows_load]:
         copy.start()
     counted = [jnp.where(there, 1, 0) for there, _ in greet]
-    for p, pair_rows in enumerate(SWAPPED):
-        kept = []
-        for side, r in enumerate(pair_rows):
-            for t in range(OWN + 1):
-                turned = spec[pl.ds(starts[t], TILE), r, :].T
-                low, high = turned[:HALF], turned[HALF:]
-                own = jnp.where(half_is0, low, high)
-                far = jnp.where(half_is0, high, low)
-                state[t, r + 1, PAD : PAD + HALF] = own
-                if t < OWN:
-                    y_out[p, 5 * side + t] = far.astype(b16)
-                else:
-                    kept.append(far)
-                if r == 3:
-                    z1_out[0, t] = own.astype(b16)
-                if r == 0:
-                    z1_out[1, t] = own.astype(b16)
-                at = 4 * t + r
-                es_out[at : at + 1] = jnp.where(row_is0, turned[127:128], turned[0:1])
-                ed_out[at : at + 1] = jnp.where(row_is0, turned[0:1], turned[127:128])
-                ep_out[at : at + 1] = jnp.where(row_is0, turned[63:64], turned[64:65])
-                el[at : at + 1] = jnp.where(row_is0, turned[64:65], turned[63:64])
-            if r == 3:
-                pl.semaphore_wait(barrier, 1 + sum(counted))
-            if side == 0:
-                swap[p][0].start()
-            if r == 3:
-                when(has_n, z1_n.start)
-            if r == 0:
-                when(has_s, z1_s.start)
-        y_out[p, 4] = pack(kept[0], kept[1], is_low)
-        swap[p][1].start()
-    when(has_same, e_same.start)
+
+    def y_slot(p, side, t):
+        if p == 0:
+            return (7, 8, 5, 6)[t] if side else t
+        return 1 + 2 * t + side
+
+    def turn(p, side, t):
+        r = SWAPPED[p][side]
+        turned = spec[pl.ds(starts[t], TILE), r, :].T
+        low, high = turned[:HALF], turned[HALF:]
+        own = jnp.where(half_is0, low, high)
+        far = jnp.where(half_is0, high, low)
+        state[t, r + 1, PAD : PAD + HALF] = own
+        if t < OWN:
+            y_out[p, y_slot(p, side, t)] = far.astype(b16)
+        if r == 3:
+            z1_out[0, t] = own.astype(b16)
+        if r == 0:
+            z1_out[1, t] = own.astype(b16)
+        at = 4 * t + r
+        es_out[at : at + 1] = jnp.where(row_is0, turned[127:128], turned[0:1])
+        ed_out[at : at + 1] = jnp.where(row_is0, turned[0:1], turned[127:128])
+        ep_out[at : at + 1] = jnp.where(row_is0, turned[63:64], turned[64:65])
+        el[at : at + 1] = jnp.where(row_is0, turned[64:65], turned[63:64])
+        return far
+
+    for side in range(2):
+        for t in (0, 1):
+            turn(0, side, t)
+        if side == 0:
+            pl.semaphore_wait(barrier, 1 + sum(counted))
+        swap[0][side].start()
+    for side in range(2):
+        for t in (2, 3):
+            turn(0, side, t)
+    y_out[0, 4] = pack(turn(0, 0, 4), turn(0, 1, 4), is_low)
+    swap[0][2].start()
+    swap[0][3].start()
+    when(has_n, z1_n.start)
+    when(has_s, z1_s.start)
+    for t in range(OWN):
+        for side in range(2):
+            turn(1, side, t)
+    y_out[1, 0] = pack(turn(1, 0, 4), turn(1, 1, 4), is_low)
+    swap[1][0].start()
     when(has_far, e_diag.start)
     e_pair.start()
+    swap[1][1].start()
+    when(has_same, e_same.start)
 
     ocean_load.wait()
     oz_out[0] = oc[:, ROWS - 1, :]
@@ -360,7 +386,7 @@
                     sums[q, cell, :] = totals[q]
             return carry
 
-        lax.fori_loop(0, 2, body, 0)
+        lax.fori_loop(0, 2, body, 0, unroll=True)
 
     def finish_sums(rows):
         total = STEPS * comps
@@ -399,6 +425,10 @@
     whole = slice(0, CELLS)
     halves = (slice(0, CELLS // 2), slice(CELLS // 2, CELLS))
 
+    swap[0][0].wait_recv()
+    when(has_n, zf_n[0].start)
+    swap[0][1].wait_recv()
+    when(has_s, zf_s[0].start)
     when(has_s, z1_n.wait_recv)
     when(has_n, z1_s.wait_recv)
     when(has_far, e_same.wait_recv)
@@ -411,10 +441,10 @@
                 state[t, 5 * d, PAD : PAD + HALF] = z1_in[d, t].astype(f32)
     for h in range(2):
         propagate(range(OWN), h, True, True)
-    swap[0][0].wait_recv()
-    swap[0][1].wait_recv()
-    when(has_n, zf_n.start)
-    when(has_s, zf_s.start)
+    swap[0][2].wait_recv()
+    when(has_n, zf_n[1].start)
+    swap[0][3].wait_recv()
+    when(has_s, zf_s[1].start)
     for copy in w1_loads:
         copy.wait()
     for n in range(4):
@@ -459,16 +489,32 @@
         tendency = mixed + jnp.concatenate([du, dv, dtemp, dsalt], axis=0)
         o_out[:, r, :] = here + msk[r : r + 1, :].astype(f32) * tendency
 
-    for p, pair_rows in enumerate(SWAPPED):
-        if p == 1:
-            swap[1][0].wait_recv()
-            swap[1][1].wait_recv()
-        for side, r in enumerate(pair_rows):
+
+    def merge(p, side, r):
+        packed = y_in[p, 4 if p == 0 else 0]
+        state[4, r + 1, PAD : PAD + HALF] = jnp.where(
+            mine, state[4, r + 1, PAD : PAD + HALF], unpack(packed, side, is_high)
+        )
+
+    def arrived(p, side, r, t):
+        state[5 + t, r + 1, PAD : PAD + HALF] = y_in[p, y_slot(p, side, t)].astype(f32)
+
+    for side, r in enumerate(SWAPPED[0]):
+        for t in range(OWN):
+            arrived(0, side, r, t)
+        merge(0, side, r)
+    for d, there, copy in ((0, has_s, zf_n), (1, has_n, zf_s)):
+        @pl.when(there)
+        def _(d=d, copy=copy):
+            for one in copy:
+                one.wait_recv()
             for t in range(OWN):
-                state[5 + t, r + 1, PAD : PAD + HALF] = y_in[p, 5 * side + t].astype(f32)
-            state[4, r + 1, PAD : PAD + HALF] = jnp.where(
-                mine, state[4, r + 1, PAD : PAD + HALF], unpack(y_in[p, 4], side, is_high)
+                at = (3, 4, 1, 2)[t] if d else t
+                state[5 + t, 5 * d, PAD : PAD + HALF] = zf_in[d, at].astype(f32)
+            state[4, 5 * d, PAD : PAD + HALF] = jnp.where(
+                mine, z1_in[d, 4].astype(f32), unpack(zf_in[d, 4 - 4 * d], d, is_high)
             )
+    swap[1][0].wait_recv()
     when(has_far, e_diag.wait_recv)
     e_pair.wait_recv()
     for t in range(OWN):
@@ -479,73 +525,82 @@
         jnp.where(mine[:4], el[16:20], ep_in[16:20]),
         jnp.where(mine[:4], es_in[16:20], ed_in[16:20]),
     )
-    for d, there, copy in ((0, has_s, zf_n), (1, has_n, zf_s)):
-        @pl.when(there)
-        def _(d=d, copy=copy):
-            copy.wait_recv()
-            for t in range(OWN):
-                state[5 + t, 5 * d, PAD : PAD + HALF] = zf_in[d, t + d].astype(f32)
-            state[4, 5 * d, PAD : PAD + HALF] = jnp.where(
-                mine, z1_in[d, 4].astype(f32), unpack(zf_in[d, 4 - 4 * d], d, is_high)
-            )
+    for side, r in enumerate(SWAPPED[1]):
+        for t in (0, 1):
+            arrived(1, side, r, t)
+        merge(1, side, r)
     for h in range(2):
-        propagate(range(OWN, TILES), h, False, False)
+        propagate((4, 5, 6), h, False, False)
+    early = slice(TILE * 4, TILE * 7)
+    late = slice(TILE * 7, TILE * 9)
+    for n in range(4):
+        lanes = slice(256 * n, 256 * (n + 1))
+        part[:, lanes] = part[:, lanes] + dot(p16[:, early], w1[early, lanes])
+    swap[1][1].wait_recv()
+    for side, r in enumerate(SWAPPED[1]):
+        for t in (2, 3):
+            arrived(1, side, r, t)
+    for h in range(2):
+        propagate((7, 8), h, False, False)
     finish_sums(whole)
     for n in range(4):
         lanes = slice(256 * n, 256 * (n + 1))
-        pre = part[:, lanes] + dot(p16[:, TILE * OWN :], w1[TILE * OWN :, lanes])
-        activate(n, pre, whole)
+        activate(n, part[:, lanes] + dot(p16[:, late], w1[late, lanes]), whole)
     for copy in w2_loads:
         copy.wait()
-    for g, tiles in enumerate(GROUPS):
-        for j, t, fresh in update(tiles, whole):
-            for n, r in enumerate(ORDER):
-                block = fresh[HALF * n : HALF * (n + 1)]
-                state[t, r + 1, PAD : PAD + HALF] = block
-                begin, end = block[:1], block[HALF - 1 :]
-                at = 4 * j + r
-                e2d_out[g, at : at + 1] = jnp.where(row_is0, begin, end)
-                e2p_out[g, at : at + 1] = jnp.where(row_is0, end, begin)
-                if r == ROWS - 1:
-                    z2_out[0, t] = block.astype(b16)
-                if r == 0:
-                    z2_out[1, t] = block.astype(b16)
+    for g, products in enumerate(PRODUCTS):
+        for tiles in products:
+            for _, t, fresh in update(tiles, whole):
+                for n, r in enumerate(ORDER):
+                    block = fresh[HALF * n : HALF * (n + 1)]
+                    state[t, r + 1, PAD : PAD + HALF] = block
+                    begin, end = block[:1], block[HALF - 1 :]
+                    at = 4 * GROUPS[g].index(t) + r
+                    e2d_out[g, at : at + 1] = jnp.where(row_is0, begin, end)
+                    e2p_out[g, at : at + 1] = jnp.where(row_is0, end, begin)
+                    if r == ROWS - 1:
+                        z2_out[0, PLACED.index(t)] = block.astype(b16)
+                    if r == 0:
+                        z2_out[1, PLACED.index(t)] = block.astype(b16)
+        e2[g][1].start()
         when(has_far, e2[g][0].start)
-        e2[g][1].start()
         when(has_n, z2[g][0].start)
         when(has_s, z2[g][1].start)
 
-    def last_updates(h):
+    def last_update(h, tiles):
         rows = halves[h]
-        for tiles in LAST_GROUPS:
-            for j, t, fresh in update(tiles, rows):
-                upper, under = fresh[:HALF], fresh[HALF:]
-                if t > OWN:
-                    at = 1 + 2 * (t - 5)
-                    f_out[h, at] = upper.astype(b16)
-                    f_out[h, at + 1] = under.astype(b16)
-                if t == OWN:
-                    f_out[h, 0] = pack(upper, under, is_high)
-                if t <= OWN:
-                    done[t, rows] = fresh
-            if tiles == (5, 6):
-                final[h][0].start()
-            if tiles == (7, 8):
-                for copy in final[h][1:]:
-                    copy.start()
+        for _, t, fresh in update(tiles, rows):
+            upper, under = fresh[:HALF], fresh[HALF:]
+            if t > OWN:
+                at = 2 * (t - 5)
+                f_out[h, at] = upper.astype(b16)
+                f_out[h, at + 1] = under.astype(b16)
+            if t == OWN:
+                f_out[h, 8] = pack(upper, under, is_high)
+            if t <= OWN:
+                done[t, rows] = fresh
+
+    def last_sends(h):
+        last_update(h, (5, 6))
+        final[h][0].start()
+        last_update(h, (7, 8))
+        if h == 1:
+            final[h][1].start()
+        last_update(h, (4,))
+        final[h][-1].start()
 
     for g, tiles in enumerate(GROUPS):
-        when(has_far, e2[SENDERS[g]][0].wait_recv)
-        e2[SENDERS[g]][1].wait_recv()
-        for j, t in enumerate(tiles):
-            lines = slice(4 * j, 4 * j + 4)
-            edges(t, e2p_in[g, lines], e2d_in[g, lines])
+        e2[g][1].wait_recv()
+        when(has_far, e2[g][0].wait_recv)
+        for t in tiles:
+            at = 4 * tiles.index(mirror(t))
+            edges(t, e2p_in[g, at : at + 4], e2d_in[g, at : at + 4])
         propagate(tiles, 0, g == 0, False)
     finish_sums(halves[0])
     for n in range(4):
         lanes = slice(256 * n, 256 * (n + 1))
         activate(n, dot(p16[halves[0]], w1[:, lanes]), halves[0])
-    last_updates(0)
+    last_sends(0)
 
     for g, tiles in enumerate(GROUPS):
         for d, there in ((0, has_s), (1, has_n)):
@@ -553,7 +608,7 @@
             def _(d=d, g=g, tiles=tiles):
                 z2[g][d].wait_recv()
                 for t in tiles:
-                    state[t, 5 * d, PAD : PAD + HALF] = z2_in[d, t].astype(f32)
+                    state[t, 5 * d, PAD : PAD + HALF] = z2_in[d, PLACED.index(t)].astype(f32)
         propagate(tiles, 1, g == 0, False)
     finish_sums(halves[1])
     scale = 1.0 / (STEPS * STEPS * comps)
@@ -567,23 +622,26 @@
     small_t[...] = small[...].T
     st_out[...] = small_t[0:8]
     stress_pair.start()
+    when(has_n, stress_n.start, stress_on.start)
+    when(has_s, stress_s.start, stress_os.start)
     for n in range(4):
         lanes = slice(256 * n, 256 * (n + 1))
         activate(n, dot(p16[halves[1]], w1[:, lanes]), halves[1])
-    last_updates(1)
+    last_sends(1)
+    for h in range(2):
+        for tiles in ((0, 1), (2, 3)):
+            last_update(h, tiles)
     stress_pair.wait_recv()
     st_full[...] = st_out[...] + st_in[...]
-    when(has_n, stress_n.start)
-    when(has_s, stress_s.start)
 
     def turn_back(h, t):
         for side in range(2):
             n = 2 * h + side
             own = done[t, HALF * n : HALF * (n + 1)]
             if t < OWN:
-                came = f_in[h, 1 + 2 * t + side].astype(f32)
+                came = f_in[h, 2 * t + side].astype(f32)
             else:
-                came = unpack(f_in[h, 0], side, is_low)
+                came = unpack(f_in[h, 8], side, is_low)
             turned = jnp.concatenate(
                 [jnp.where(half_is0, own, came), jnp.where(half_is0, came, own)], axis=0
             ).T
@@ -596,20 +654,21 @@
                 )
 
     final[0][0].wait_recv()
-    for t in (4, 0, 1):
+    for t in (0, 1):
         turn_back(0, t)
     final[0][1].wait_recv()
-    for t in (2, 3):
+    for t in (2, 3, 4):
         turn_back(0, t)
 
     sb_load.wait()
     srows_load.wait()
-    when(has_s, stress_n.wait_recv)
-    when(has_n, stress_s.wait_recv)
+    when(has_s, stress_n.wait_recv, stress_on.wait_recv)
+    when(has_n, stress_s.wait_recv, stress_os.wait_recv)
+    beyond = [sz_in[d] + sx_in[d] for d in range(2)]
     for k in range(2):
-        lines = [sz_in[0, 4 * k + 3 : 4 * k + 4]]
+        lines = [beyond[0][4 * k + 3 : 4 * k + 4]]
         lines += [st_full[4 * k + r : 4 * k + r + 1] for r in range(ROWS)]
-        lines += [sz_in[1, 4 * k : 4 * k + 1]]
+        lines += [beyond[1][4 * k : 4 * k + 1]]
         for r in range(ROWS):
             total = sb[r, 0] * choose(srows, r, 0, *lines[r : r + 3])
             total = total + sb[r, 1] * choose(srows, r, 1, *lines[r : r + 3])
@@ -618,13 +677,16 @@
             at = 16 * k
             o_out[at : at + 1, r, :] = o_out[at : at + 1, r, :] + wet * (STRESS_GAIN * stress)
 
-    for n, tiles in enumerate(((4, 0, 1), (2,), (3,))):
+    for n, tiles in enumerate(((0, 1), (2, 3), (4,))):
         final[1][n].wait_recv()
         for t in tiles:
             turn_back(1, t)
 
-    when(has_n, ocean_n.wait_send, z1_n.wait_send, zf_n.wait_send, stress_n.wait_send)
-    when(has_s, ocean_s.wait_send, z1_s.wait_send, zf_s.wait_send, stress_s.wait_send)
+    when(has_n, ocean_n.wait_send, z1_n.wait_send, stress_n.wait_send, stress_on.wait_send)
+    when(has_s, ocean_s.wait_send, z1_s.wait_send, stress_s.wait_send, stress_os.wait_send)
+    for n in range(2):
+        when(has_n, zf_n[n].wait_send)
+        when(has_s, zf_s[n].wait_send)
     when(has_e, ocean_e.wait_send)
     when(has_w, ocean_w.wait_send)
     when(has_same, e_same.wait_send)
@@ -680,7 +742,7 @@
         *[vmem((24, TILE), f32) for _ in range(7)],
         vmem((2, TILES, HALF, TILE), b16),
         vmem((2, TILES, HALF, TILE), b16),
-        *[vmem((groups, 8, TILE), f32) for _ in range(4)],
+        *[vmem((groups, 24, TILE), f32) for _ in range(4)],
         vmem((2, 64, COLS), f32),
         vmem((2, 64, COLS), f32),
         vmem((256, COLS), f32),
@@ -690,6 +752,7 @@
         vmem((8, COLS), f32),
         vmem((8, COLS), f32),
         vmem((2, 8, COLS), f32),
+        vmem((2, 8, COLS), f32),
         vmem((2, TILES, HALF, TILE), b16),
         vmem((2, TILES, HALF, TILE), b16),
         vmem((OWN + 1, CELLS, TILE), f32),
@@ -698,13 +761,13 @@
         dma((15,)),
         dma((2,)), dma((2,)),
         dma((2,)), dma((2,)),
+        dma((2, 4)), dma((2, 4)),
+        dma((2,)), dma((2,)),
         dma((2, 2)), dma((2, 2)),
-        dma((2,)), dma((2,)),
-        dma((2,)), dma((2,)),
         dma((3,)), dma((3,)),
         dma((2, groups)), dma((2, groups)),
         dma((2, groups)), dma((2, groups)),
-        dma((3,)), dma((3,)),
+        dma((5,)), dma((5,)),
         dma((2, 3)), dma((2, 3)),
     ]
     return pl.pallas_call(

time: 32.8 us -> 31.4 us (0.957)
  Pallas kernels: 32 us -> 30.6 us
    pallas_call x1, Pallas kernels: 30.9 us -> 29.5 us  [kernel_call(): pl.pallas_call(kernel, out_shape=(shape(spectra.shape, f32), shape(ocean....]
where the time goes in v2:
time: 31.4 us; the launch traced here: 31.2 us
  Pallas kernels  30.6 us (97%)
  between operations  0.64 us (2%)
    pallas_call x1, Pallas kernels, kernel_call(): pl.pallas_call(kernel, out_shape=(shape(spectra.shape, f32), shape(ocean....  29.5 us
    pallas_call x1, Pallas kernels, place_call(): pl.pallas_call(place_kernel, out_shape=(shape(a.shape, a.dtype), shape(b....  1.09 us

profile of v2, /device:TPU:0, one launch (start us, length us, event | category | flops | bytes accessed | tf_op | source)
XLA Modules:
  0.0 31.2 jit_solution(13267896943806656582)
XLA Ops:
  0.6 29.5 %shard_map.122 = (f32[576,4,128]{2,1,0:T(4,128)S(1)}, f32[64,4,128]{2,1,0:T(4,128)S(1)}) custom-call(f32[576,4,128]{2,1,0:T(4,128)} %bitcast.6, bf16[1152,1024]{1,0:T(8,128)(2,1)} %first.1, bf16[1024,1152]{1,0:T(8,128)(2,1)} %second.1, f32[2,9,8,128]{3,2,1,0:T(8,128)} %constant.2.clone.table, f32[64,4,128]{2,1,0:T(4,128)} %bitcast.7, f32[2,4,128]{2,1,0:T(4,128)} %wind.1, ...), custom_call_target="tpu_custom_call" | custom-call | tf_op jit(solution)/shard_map/pallas_call | solution.py:773
  30.1 1.1 %shard_map.123 = (f32[576,4,128]{2,1,0:T(4,128)}, f32[64,4,128]{2,1,0:T(4,128)}) custom-call(f32[576,4,128]{2,1,0:T(4,128)S(1)} %get-tuple-element.6.a, f32[64,4,128]{2,1,0:T(4,128)S(1)} %get-tuple-element.7.b), custom_call_target="tpu_custom_call" | custom-call | tf_op jit(solution)/shard_map/pallas_call | solution.py:807

commit v3 on v2

--- a/solution.py
+++ b/solution.py
@@ -70,7 +70,7 @@
     spectra, first, second, table, ocean, wind, mask, cblocks, sblocks, crows_in, srows_in,
     out, o_out,
     spec, w1, w2, tab, oc, wnd, msk, cb, sb,
-    state, prop, rate, p16, part, hidden, sums, cells, gain, back, squared, small, small_t,
+    state, later, prop, rate, p16, part, hidden, sums, cells, gain, back, squared, small, small_t,
     y_out, y_in, z1_out, z1_in, zf_in, es_out, es_in, ed_out, ed_in, ep_out, ep_in, el,
     z2_out, z2_in, e2d_out, e2d_in, e2p_out, e2p_in,
     oz_out, oz_in, ocat, ox_out, ox_in, st_out, st_in, st_full, sz_in, sx_in, f_out, f_in, done,
@@ -189,9 +189,11 @@
             )
             for d in range(2)
         ])
+
+    for h in range(2):
         e2.append([
-            remote(e2d_out.at[g], e2d_in.at[g], e2_send.at[0, g], e2_recv.at[0, g], diag),
-            remote(e2p_out.at[g], e2p_in.at[g], e2_send.at[1, g], e2_recv.at[1, g], pair),
+            remote(e2d_out.at[h], e2d_in.at[h], e2_send.at[0, h], e2_recv.at[0, h], diag),
+            remote(e2p_out.at[h], e2p_in.at[h], e2_send.at[1, h], e2_recv.at[1, h], pair),
         ])
     stress_pair = remote(st_out, st_in, s_send.at[0], s_recv.at[0], pair)
     stress_n = remote(st_out, sz_in.at[0], s_send.at[1], s_recv.at[1], north)
@@ -216,7 +218,8 @@
                 action()
 
     for edge in (0, ROWS + 1):
-        state[:, edge, PAD : PAD + HALF] = jnp.zeros((TILES, HALF, TILE), f32)
+        for field in (state, later):
+            field[:, edge, PAD : PAD + HALF] = jnp.zeros((TILES, HALF, TILE), f32)
     spec[:HALF] = jnp.zeros((HALF, ROWS, COLS), f32)
     spec[HALF + comps :] = jnp.zeros((HALF, ROWS, COLS), f32)
 
@@ -342,13 +345,13 @@
                 CURRENT_GAIN * total.sum(axis=1, keepdims=True), (HALF, TILE)
             )
 
-    def edges(t, pair_side, far_side):
-        for r in range(ROWS):
-            near, far = pair_side[r : r + 1], far_side[r : r + 1]
-            state[t, r + 1, PAD - 1 : PAD] = jnp.where(row_is0, far, near)
-            state[t, r + 1, PAD + HALF : PAD + HALF + 1] = jnp.where(row_is0, near, far)
-
-    def propagate(tiles, h, fresh, fresh_push):
+    def edges(field, t, rows, pair_side, far_side):
+        for n, r in enumerate(rows):
+            near, away = pair_side[n : n + 1], far_side[n : n + 1]
+            field[t, r + 1, PAD - 1 : PAD] = jnp.where(row_is0, away, near)
+            field[t, r + 1, PAD + HALF : PAD + HALF + 1] = jnp.where(row_is0, near, away)
+
+    def propagate(field, tiles, h, fresh, fresh_push):
         def body(i, carry):
             at = pl.multiple_of((2 * h + i) * HALF, HALF)
             r = 3 * i if h else 1 + i
@@ -365,11 +368,11 @@
                         tab[t, q : q + 1, :] for q in range(6)
                     )
                     top = PAD + lo
-                    here = state[t, r + 1, top : top + 32]
-                    before = state[t, r + 1, top - 1 : top + 31]
-                    after = state[t, r + 1, top + 1 : top + 33]
-                    below = state[t, r, top : top + 32]
-                    above = state[t, r + 2, top : top + 32]
+                    here = field[t, r + 1, top : top + 32]
+                    before = field[t, r + 1, top - 1 : top + 31]
+                    after = field[t, r + 1, top + 1 : top + 33]
+                    below = field[t, r, top : top + 32]
+                    above = field[t, r + 2, top : top + 32]
                     cx = speed_x + cur_x
                     cy = speed_y + cur_y
                     flux = jnp.abs(cx) * (here - jnp.where(cx > 0.0, before, after))
@@ -433,14 +436,14 @@
     when(has_n, z1_s.wait_recv)
     when(has_far, e_same.wait_recv)
     for t in range(OWN):
-        edges(t, el[4 * t : 4 * t + 4], es_in[4 * t : 4 * t + 4])
+        edges(state, t, range(4), el[4 * t : 4 * t + 4], es_in[4 * t : 4 * t + 4])
     for d, there in ((0, has_s), (1, has_n)):
         @pl.when(there)
         def _(d=d):
             for t in range(OWN):
                 state[t, 5 * d, PAD : PAD + HALF] = z1_in[d, t].astype(f32)
     for h in range(2):
-        propagate(range(OWN), h, True, True)
+        propagate(state, range(OWN), h, True, True)
     swap[0][2].wait_recv()
     when(has_n, zf_n[1].start)
     swap[0][3].wait_recv()
@@ -503,6 +506,65 @@
         for t in range(OWN):
             arrived(0, side, r, t)
         merge(0, side, r)
+    swap[1][0].wait_recv()
+    when(has_far, e_diag.wait_recv)
+    e_pair.wait_recv()
+    for t in range(OWN):
+        lines = slice(4 * t, 4 * t + 4)
+        edges(state, 5 + t, range(4), ep_in[lines], ed_in[lines])
+    edges(
+        state,
+        4,
+        range(4),
+        jnp.where(mine[:4], el[16:20], ep_in[16:20]),
+        jnp.where(mine[:4], es_in[16:20], ed_in[16:20]),
+    )
+    for side, r in enumerate(SWAPPED[1]):
+        for t in (0, 1):
+            arrived(1, side, r, t)
+        merge(1, side, r)
+    propagate(state, (4, 5, 6), 0, False, False)
+    early = slice(TILE * 4, TILE * 7)
+    late = slice(TILE * 7, TILE * 9)
+    for n in range(4):
+        lanes = slice(256 * n, 256 * (n + 1))
+        extra = dot(p16[halves[0], early], w1[early, lanes])
+        part[halves[0], lanes] = part[halves[0], lanes] + extra
+    swap[1][1].wait_recv()
+    for side, r in enumerate(SWAPPED[1]):
+        for t in (2, 3):
+            arrived(1, side, r, t)
+    propagate(state, (7, 8), 0, False, False)
+
+    def first_network(h, taken):
+        rows = halves[h]
+        finish_sums(rows)
+        for n in range(4):
+            lanes = slice(256 * n, 256 * (n + 1))
+            activate(n, part[rows, lanes] + dot(p16[rows, taken], w1[taken, lanes]), rows)
+
+    def first_update(h, products):
+        for tiles in products:
+            for _, t, fresh in update(tiles, halves[h]):
+                for side in range(2):
+                    r = ORDER[2 * h + side]
+                    block = fresh[HALF * side : HALF * (side + 1)]
+                    later[t, r + 1, PAD : PAD + HALF] = block
+                    begin, end = block[:1], block[HALF - 1 :]
+                    at = 2 * PLACED.index(t) + side
+                    e2d_out[h, at : at + 1] = jnp.where(row_is0, begin, end)
+                    e2p_out[h, at : at + 1] = jnp.where(row_is0, end, begin)
+                    if r == ROWS - 1:
+                        z2_out[0, PLACED.index(t)] = block.astype(b16)
+                    if r == 0:
+                        z2_out[1, PLACED.index(t)] = block.astype(b16)
+
+    for copy in w2_loads:
+        copy.wait()
+    first_network(0, late)
+    first_update(0, PRODUCTS[0] + PRODUCTS[1])
+    e2[0][1].start()
+    when(has_far, e2[0][0].start)
     for d, there, copy in ((0, has_s, zf_n), (1, has_n, zf_s)):
         @pl.when(there)
         def _(d=d, copy=copy):
@@ -514,58 +576,16 @@
             state[4, 5 * d, PAD : PAD + HALF] = jnp.where(
                 mine, z1_in[d, 4].astype(f32), unpack(zf_in[d, 4 - 4 * d], d, is_high)
             )
-    swap[1][0].wait_recv()
-    when(has_far, e_diag.wait_recv)
-    e_pair.wait_recv()
-    for t in range(OWN):
-        lines = slice(4 * t, 4 * t + 4)
-        edges(5 + t, ep_in[lines], ed_in[lines])
-    edges(
-        4,
-        jnp.where(mine[:4], el[16:20], ep_in[16:20]),
-        jnp.where(mine[:4], es_in[16:20], ed_in[16:20]),
-    )
-    for side, r in enumerate(SWAPPED[1]):
-        for t in (0, 1):
-            arrived(1, side, r, t)
-        merge(1, side, r)
-    for h in range(2):
-        propagate((4, 5, 6), h, False, False)
-    early = slice(TILE * 4, TILE * 7)
-    late = slice(TILE * 7, TILE * 9)
-    for n in range(4):
-        lanes = slice(256 * n, 256 * (n + 1))
-        part[:, lanes] = part[:, lanes] + dot(p16[:, early], w1[early, lanes])
-    swap[1][1].wait_recv()
-    for side, r in enumerate(SWAPPED[1]):
-        for t in (2, 3):
-            arrived(1, side, r, t)
-    for h in range(2):
-        propagate((7, 8), h, False, False)
-    finish_sums(whole)
-    for n in range(4):
-        lanes = slice(256 * n, 256 * (n + 1))
-        activate(n, part[:, lanes] + dot(p16[:, late], w1[late, lanes]), whole)
-    for copy in w2_loads:
-        copy.wait()
-    for g, products in enumerate(PRODUCTS):
-        for tiles in products:
-            for _, t, fresh in update(tiles, whole):
-                for n, r in enumerate(ORDER):
-                    block = fresh[HALF * n : HALF * (n + 1)]
-                    state[t, r + 1, PAD : PAD + HALF] = block
-                    begin, end = block[:1], block[HALF - 1 :]
-                    at = 4 * GROUPS[g].index(t) + r
-                    e2d_out[g, at : at + 1] = jnp.where(row_is0, begin, end)
-                    e2p_out[g, at : at + 1] = jnp.where(row_is0, end, begin)
-                    if r == ROWS - 1:
-                        z2_out[0, PLACED.index(t)] = block.astype(b16)
-                    if r == 0:
-                        z2_out[1, PLACED.index(t)] = block.astype(b16)
-        e2[g][1].start()
-        when(has_far, e2[g][0].start)
-        when(has_n, z2[g][0].start)
-        when(has_s, z2[g][1].start)
+    propagate(state, range(OWN, TILES), 1, False, False)
+    first_network(1, slice(TILE * 4, TILE * 9))
+    first_update(1, PRODUCTS[0])
+    when(has_n, z2[0][0].start)
+    when(has_s, z2[0][1].start)
+    first_update(1, PRODUCTS[1])
+    e2[1][1].start()
+    when(has_far, e2[1][0].start)
+    when(has_n, z2[1][0].start)
+    when(has_s, z2[1][1].start)
 
     def last_update(h, tiles):
         rows = halves[h]
@@ -589,27 +609,31 @@
         last_update(h, (4,))
         final[h][-1].start()
 
-    for g, tiles in enumerate(GROUPS):
-        e2[g][1].wait_recv()
-        when(has_far, e2[g][0].wait_recv)
-        for t in tiles:
-            at = 4 * tiles.index(mirror(t))
-            edges(t, e2p_in[g, at : at + 4], e2d_in[g, at : at + 4])
-        propagate(tiles, 0, g == 0, False)
+    def second_edges(h):
+        e2[h][1].wait_recv()
+        when(has_far, e2[h][0].wait_recv)
+        for t in range(TILES):
+            at = 2 * PLACED.index(mirror(t))
+            lines = slice(at, at + 2)
+            edges(later, t, ORDER[2 * h : 2 * h + 2], e2p_in[h, lines], e2d_in[h, lines])
+
+    second_edges(0)
+    propagate(later, range(TILES), 0, True, False)
     finish_sums(halves[0])
     for n in range(4):
         lanes = slice(256 * n, 256 * (n + 1))
         activate(n, dot(p16[halves[0]], w1[:, lanes]), halves[0])
     last_sends(0)
 
+    second_edges(1)
     for g, tiles in enumerate(GROUPS):
         for d, there in ((0, has_s), (1, has_n)):
             @pl.when(there)
             def _(d=d, g=g, tiles=tiles):
                 z2[g][d].wait_recv()
                 for t in tiles:
-                    state[t, 5 * d, PAD : PAD + HALF] = z2_in[d, PLACED.index(t)].astype(f32)
-        propagate(tiles, 1, g == 0, False)
+                    later[t, 5 * d, PAD : PAD + HALF] = z2_in[d, PLACED.index(t)].astype(f32)
+        propagate(later, tiles, 1, g == 0, False)
     finish_sums(halves[1])
     scale = 1.0 / (STEPS * STEPS * comps)
     packed = jnp.zeros((HALF, TILE), f32)
@@ -696,8 +720,9 @@
     for g in range(len(GROUPS)):
         when(has_n, z2[g][0].wait_send)
         when(has_s, z2[g][1].wait_send)
-        when(has_far, e2[g][0].wait_send)
-        e2[g][1].wait_send()
+    for h in range(2):
+        when(has_far, e2[h][0].wait_send)
+        e2[h][1].wait_send()
 
 
 def kernel_call(
@@ -722,6 +747,7 @@
         vmem((ROWS, 2, HALF, COLS), f32),
         vmem((ROWS, 2, COLS, COLS), f32),
         vmem((TILES, ROWS + 2, HALF + 2 * PAD, TILE), f32),
+        vmem((TILES, ROWS + 2, HALF + 2 * PAD, TILE), f32),
         vmem((TILES, CELLS, TILE), f32),
         vmem((TILES, CELLS, TILE), f32),
         vmem((CELLS, total), b16),
@@ -742,7 +768,7 @@
         *[vmem((24, TILE), f32) for _ in range(7)],
         vmem((2, TILES, HALF, TILE), b16),
         vmem((2, TILES, HALF, TILE), b16),
-        *[vmem((groups, 24, TILE), f32) for _ in range(4)],
+        *[vmem((2, 24, TILE), f32) for _ in range(4)],
         vmem((2, 64, COLS), f32),
         vmem((2, 64, COLS), f32),
         vmem((256, COLS), f32),

time: 31.4 us -> 28.7 us (0.914)
  Pallas kernels: 30.6 us -> 27.9 us
    pallas_call x1, Pallas kernels: 29.5 us -> 26.8 us  [kernel_call(): pl.pallas_call(kernel, out_shape=(shape(spectra.shape, f32), shape(ocean....]
where the time goes in v3:
time: 28.7 us; the launch traced here: 28.5 us
  Pallas kernels  27.9 us (97%)
  between operations  0.64 us (2%)
    pallas_call x1, Pallas kernels, kernel_call(): pl.pallas_call(kernel, out_shape=(shape(spectra.shape, f32), shape(ocean....  26.8 us
    pallas_call x1, Pallas kernels, place_call(): pl.pallas_call(place_kernel, out_shape=(shape(a.shape, a.dtype), shape(b....  1.09 us

profile of v3, /device:TPU:0, one launch (start us, length us, event | category | flops | bytes accessed | tf_op | source)
XLA Modules:
  0.0 28.5 jit_solution(133399543010459733)
XLA Ops:
  0.6 26.8 %shard_map.122 = (f32[576,4,128]{2,1,0:T(4,128)S(1)}, f32[64,4,128]{2,1,0:T(4,128)S(1)}) custom-call(f32[576,4,128]{2,1,0:T(4,128)} %bitcast.6, bf16[1152,1024]{1,0:T(8,128)(2,1)} %first.1, bf16[1024,1152]{1,0:T(8,128)(2,1)} %second.1, f32[2,9,8,128]{3,2,1,0:T(8,128)} %constant.2.clone.table, f32[64,4,128]{2,1,0:T(4,128)} %bitcast.7, f32[2,4,128]{2,1,0:T(4,128)} %wind.1, ...), custom_call_target="tpu_custom_call" | custom-call | tf_op jit(solution)/shard_map/pallas_call | solution.py:799
  27.5 1.1 %shard_map.123 = (f32[576,4,128]{2,1,0:T(4,128)}, f32[64,4,128]{2,1,0:T(4,128)}) custom-call(f32[576,4,128]{2,1,0:T(4,128)S(1)} %get-tuple-element.6.a, f32[64,4,128]{2,1,0:T(4,128)S(1)} %get-tuple-element.7.b), custom_call_target="tpu_custom_call" | custom-call | tf_op jit(solution)/shard_map/pallas_call | solution.py:833

commit v4 on v3

--- a/solution.py
+++ b/solution.py
@@ -92,7 +92,11 @@
     own_at = pl.multiple_of(me * 5 * TILE, TILE)
     far_at = pl.multiple_of(other * 5 * TILE, TILE)
     half_at = pl.multiple_of(me * HALF, HALF)
-    spec_load = local(spectra, spec.at[pl.ds(HALF, comps)], 0)
+    cut = HALF + 2 * TILE
+    spec_load = local(spectra.at[pl.ds(0, cut)], spec.at[pl.ds(HALF, cut)], 0)
+    spec_rest = local(
+        spectra.at[pl.ds(cut, comps - cut)], spec.at[pl.ds(HALF + cut, comps - cut)], 15
+    )
     ocean_load = local(ocean, oc, 1)
     wind_load = local(wind, wnd, 2)
     mask_load = local(mask, msk, 3)
@@ -111,7 +115,7 @@
     ]
     crows_load = local(crows_in, crows, 13)
     srows_load = local(srows_in, srows, 14)
-    for copy in (spec_load, ocean_load, wind_load, mask_load, table_load, crows_load):
+    for copy in (spec_load, spec_rest, ocean_load, wind_load, mask_load, table_load, crows_load):
         copy.start()
 
     for ref in (es_in, ed_in, e2d_in, sz_in, sx_in, ox_in, oz_in):
@@ -243,8 +247,6 @@
     is_low, is_high = half_is0, jnp.logical_not(half_is0)
     starts = [HALF + me * HALF + TILE * t for t in range(OWN)] + [other * (comps + HALF - 64)]
     spec_load.wait()
-    for copy in [cb_load] + w1_loads + w2_loads + [sb_load, srows_load]:
-        copy.start()
     counted = [jnp.where(there, 1, 0) for there, _ in greet]
 
     def y_slot(p, side, t):
@@ -278,6 +280,9 @@
         if side == 0:
             pl.semaphore_wait(barrier, 1 + sum(counted))
         swap[0][side].start()
+    spec_rest.wait()
+    for copy in [cb_load] + w1_loads + w2_loads + [sb_load, srows_load]:
+        copy.start()
     for side in range(2):
         for t in (2, 3):
             turn(0, side, t)
@@ -784,7 +789,7 @@
         vmem((OWN + 1, CELLS, TILE), f32),
         pltpu.SMEM((2, 1, ROWS), jnp.int32),
         pltpu.SMEM((2, 1, ROWS), jnp.int32),
-        dma((15,)),
+        dma((16,)),
         dma((2,)), dma((2,)),
         dma((2,)), dma((2,)),
         dma((2, 4)), dma((2, 4)),

time: 28.7 us -> 28.6 us (level)
  no operation moved by 1% of the time
where the time goes in v4:
time: 28.6 us; the launch traced here: 28.5 us
  Pallas kernels  27.8 us (97%)
  between operations  0.64 us (2%)
    pallas_call x1, Pallas kernels, kernel_call(): pl.pallas_call(kernel, out_shape=(shape(spectra.shape, f32), shape(ocean....  26.7 us
    pallas_call x1, Pallas kernels, place_call(): pl.pallas_call(place_kernel, out_shape=(shape(a.shape, a.dtype), shape(b....  1.09 us

profile of v4, /device:TPU:0, one launch (start us, length us, event | category | flops | bytes accessed | tf_op | source)
XLA Modules:
  0.0 28.5 jit_solution(16384444266291584382)
XLA Ops:
  0.6 26.7 %shard_map.122 = (f32[576,4,128]{2,1,0:T(4,128)S(1)}, f32[64,4,128]{2,1,0:T(4,128)S(1)}) custom-call(f32[576,4,128]{2,1,0:T(4,128)} %bitcast.6, bf16[1152,1024]{1,0:T(8,128)(2,1)} %first.1, bf16[1024,1152]{1,0:T(8,128)(2,1)} %second.1, f32[2,9,8,128]{3,2,1,0:T(8,128)} %constant.2.clone.table, f32[64,4,128]{2,1,0:T(4,128)} %bitcast.7, f32[2,4,128]{2,1,0:T(4,128)} %wind.1, ...), custom_call_target="tpu_custom_call" | custom-call | tf_op jit(solution)/shard_map/pallas_call | solution.py:804
  27.4 1.1 %shard_map.123 = (f32[576,4,128]{2,1,0:T(4,128)}, f32[64,4,128]{2,1,0:T(4,128)}) custom-call(f32[576,4,128]{2,1,0:T(4,128)S(1)} %get-tuple-element.6.a, f32[64,4,128]{2,1,0:T(4,128)S(1)} %get-tuple-element.7.b), custom_call_target="tpu_custom_call" | custom-call | tf_op jit(solution)/shard_map/pallas_call | solution.py:838
